TPU v7x, 256 devices: a whole 4x4x8 slice. The times are simulated.
256 devices in a mesh: band: 64 (over z, y, core), col: 4 (over x).
Axes of the slice: x: 4, y: 4, z: 8, core: 2. Of those that a mesh axis runs over, the one named last changes fastest.
Arguments:
- prior_basis: float32 [64, 2, 4, 512, 1024], P(None, None, None, 'band', 'col'), may hold values from -0.0043945312 to 0.0043945312, as said below
- coupling: float32 [2, 4, 4, 512, 1024], P(None, None, None, 'band', 'col'), may hold values from -1.8 to 1.8
- velocity: float32 [2, 512, 1024], P(None, 'band', 'col'), may hold values from -0.5 to 1
Outputs:
- basis_next: float32 [64, 2, 4, 512, 1024], P(None, None, None, 'band', 'col')
- triangle: float32 [64, 64], replicated
Inputs may be any that keep to these rules, and one draw needn't show every extreme that they name: `prior_basis`: 64 earlier basis vectors.
All inputs are finite; a program needn't handle non-finite values.
Results may differ from a plain program's by a relative error of at most 0.0013.
Values sent between devices are 32-bit elements; how exact they have to be, the bound alone decides.
No kernel may reach another device: no remote copies, remote signals or barrier semaphores. Data moves between devices by JAX's collectives and lax.ppermute only.
A program may use at most 64 MiB of HBM per device.

v0:
```python
import math

import jax
import jax.numpy as jnp
from jax import lax
from jax.experimental import pallas as pl
from jax.experimental.pallas import tpu as pltpu
from jax.sharding import PartitionSpec as P

BLOCK = 16
STEPS = 4
KPREV = 64
COMPS = 8
ROWS = 8
COLS = 256
LANES = 128
WIDTH = 4
PLANES = COMPS * BLOCK
COUPLINGS = 32
COEFFS = 40
SLAB = PLANES + COEFFS
TILES = SLAB // 8
PACKED = (TILES + 1) // 2
SPAN = ROWS + 2 * WIDTH
WIDE = COLS + LANES
BOTH = 2 * KPREV

ANY = pl.BlockSpec(memory_space=pl.ANY)
VMEM = pl.BlockSpec(memory_space=pltpu.VMEM)


def core_of_chip():
    return lax.rem(lax.axis_index("band"), 2)


def pack_kernel(basis, coupling, velocity, slab_out, core_out, chip_out, edges, slab, sems, out_sems):
    copies = []
    for row in range(ROWS):
        for comp in range(COMPS):
            copies.append(
                pltpu.make_async_copy(
                    basis.at[pl.ds(KPREV - BLOCK, BLOCK), comp, row, :],
                    slab.at[row, pl.ds(comp * BLOCK, BLOCK), :],
                    sems.at[row, comp],
                )
            )
        copies.append(
            pltpu.make_async_copy(
                coupling.at[:, row, :],
                slab.at[row, pl.ds(PLANES, COUPLINGS), :],
                sems.at[row, COMPS],
            )
        )
    for copy in copies:
        copy.start()
    half_rows = 0.5 * velocity[0]
    half_cols = 0.5 * velocity[1]
    stencil = (0.15 - half_rows, 0.15 + half_rows, 0.15 - half_cols, 0.15 + half_cols)
    blank = jnp.zeros((4, COLS), jnp.float32)
    for row in range(ROWS):
        slab[row, PLANES + COUPLINGS :, :] = jnp.concatenate(
            [part[row : row + 1] for part in stencil] + [blank], axis=0
        )
    for copy in copies:
        copy.wait()
    core = core_of_chip()
    inner = pl.multiple_of((1 - core) * WIDTH, WIDTH)
    outer = pl.multiple_of(core * WIDTH, WIDTH)
    outs = [
        pltpu.make_async_copy(slab.at[pl.ds(inner, WIDTH)], core_out, out_sems.at[0]),
        pltpu.make_async_copy(slab.at[pl.ds(outer, WIDTH)], chip_out, out_sems.at[1]),
        pltpu.make_async_copy(slab, slab_out, out_sems.at[2]),
    ]
    for copy in outs:
        copy.start()
    lane = lax.broadcasted_iota(jnp.int32, (8, LANES), 1)
    for packed in range(PACKED):
        total = jnp.zeros((8, LANES), jnp.float32)
        for half in range(2):
            tile = 2 * packed + half
            if tile >= TILES:
                continue
            for row in range(ROWS):
                group = half * ROWS + row
                first = slab[row, tile * 8 : tile * 8 + 8, 0:LANES]
                last = slab[row, tile * 8 : tile * 8 + 8, COLS - LANES : COLS]
                edge = pltpu.roll(jnp.where(lane < WIDTH, first, last), (8 * group + 4) % LANES, 1)
                total = jnp.where(lane // 8 == group, edge, total)
        edges[packed] = total
    for copy in outs:
        copy.wait()


def operator_row(cur, nxt, coef, row, tiles):
    width = tiles * LANES

    def coeff(plane):
        return jnp.broadcast_to(coef[row, pl.ds(plane, 1), 0:width], (BLOCK, width))

    lower_c, upper_c = coeff(COUPLINGS + 1), coeff(COUPLINGS)
    right_c, left_c = coeff(COUPLINGS + 2), coeff(COUPLINGS + 3)
    center = []
    sums = []
    for comp in range(COMPS):
        planes = pl.ds(comp * BLOCK, BLOCK)
        here = cur[row, planes, :]
        right = pltpu.roll(here, WIDE - 1, 1)[:, :width]
        left = pltpu.roll(here, 1, 1)[:, :width]
        center.append(here[:, :width])
        sums.append(
            upper_c * cur[row + 1, planes, 0:width]
            + lower_c * cur[row - 1, planes, 0:width]
            + right_c * right
            + left_c * left
        )
    for field in range(4):
        real, imag = sums[field], sums[4 + field]
        for source in range(4):
            coeff_real = coeff(field * 4 + source)
            coeff_imag = coeff(16 + field * 4 + source)
            if source == field:
                coeff_real = coeff_real - 0.6
            real = real + coeff_real * center[source] - coeff_imag * center[4 + source]
            imag = imag + coeff_real * center[4 + source] + coeff_imag * center[source]
        nxt[row, pl.ds(field * BLOCK, BLOCK), 0:width] = real
        nxt[row, pl.ds((4 + field) * BLOCK, BLOCK), 0:width] = imag


def split(value):
    high = value.astype(jnp.bfloat16)
    return high, (value - high.astype(jnp.float32)).astype(jnp.bfloat16)


def power_kernel(
    basis, slab, from_core, from_chip, sides, core_sides, chip_sides,
    split_out, inner_out,
    ping, pong, coef, prior, parts, total, sems, halo_sems, out_sems,
):
    core = core_of_chip()
    is_first = core == 0
    core_at = pl.multiple_of((1 - core) * (SPAN - WIDTH), WIDTH)
    chip_at = pl.multiple_of(core * (SPAN - WIDTH), WIDTH)
    halos = []
    for index, (source, where, count) in enumerate(
        ((slab, WIDTH, ROWS), (from_core, core_at, WIDTH), (from_chip, chip_at, WIDTH))
    ):
        halos.append(
            pltpu.make_async_copy(
                source.at[:, pl.ds(0, PLANES), :],
                ping.at[pl.ds(where, count), :, pl.ds(0, COLS)],
                halo_sems.at[2 * index],
            )
        )
        halos.append(
            pltpu.make_async_copy(
                source.at[:, pl.ds(PLANES, COEFFS), :],
                coef.at[pl.ds(where, count), :, pl.ds(0, COLS)],
                halo_sems.at[2 * index + 1],
            )
        )
    for copy in halos:
        copy.start()
    copies = []
    for row in range(ROWS):
        for comp in range(COMPS):
            copies.append(
                pltpu.make_async_copy(
                    basis.at[:, comp, row, :],
                    prior.at[row, :, pl.ds(comp * COLS, COLS)],
                    sems.at[row, comp],
                )
            )
    for copy in copies:
        copy.start()
    lane = lax.broadcasted_iota(jnp.int32, (8, LANES), 1)
    near = (lane < WIDTH) | (lane >= LANES - WIDTH)
    for packed in range(PACKED):
        own = sides[packed]
        by_core, by_chip = core_sides[packed], chip_sides[packed]
        above = jnp.where(is_first, by_core, by_chip)
        below = jnp.where(is_first, by_chip, by_core)
        for half in range(2):
            tile = 2 * packed + half
            if tile >= TILES:
                continue
            for row in range(SPAN):
                if row < WIDTH:
                    source, source_row = below, row + ROWS - WIDTH
                elif row < WIDTH + ROWS:
                    source, source_row = own, row - WIDTH
                else:
                    source, source_row = above, row - WIDTH - ROWS
                group = half * ROWS + source_row
                edge = pltpu.roll(source, (2 * LANES - 8 * group - 4) % LANES, 1)
                edge = jnp.where(near, edge, 0.0)
                if tile < PLANES // 8:
                    ping[row, tile * 8 : tile * 8 + 8, COLS:WIDE] = edge
                else:
                    at = tile * 8 - PLANES
                    coef[row, at : at + 8, COLS:WIDE] = edge
    for copy in halos:
        copy.wait()
    buffers = (ping, pong)
    for step in range(1, STEPS + 1):
        cur, nxt = buffers[(step - 1) % 2], buffers[step % 2]
        tiles = 3 if step < STEPS else 2

        def one_row(row, carry, cur=cur, nxt=nxt, tiles=tiles):
            for tile in range(1):
                operator_row(cur, nxt, coef, row, tiles)
            return carry

        lax.fori_loop(step, SPAN - step, one_row, 0)

        def one_split(row, carry, nxt=nxt, step=step):
            at = KPREV + (step - 1) * BLOCK
            for comp in range(COMPS):
                high, low = split(nxt[row + WIDTH, pl.ds(comp * BLOCK, BLOCK), 0:COLS])
                parts[row, pl.ds(at, BLOCK), pl.ds(comp * COLS, COLS)] = high
                parts[row, pl.ds(BOTH + at, BLOCK), pl.ds(comp * COLS, COLS)] = low
            return carry

        lax.fori_loop(0, ROWS, one_split, 0)
    for copy in copies:
        copy.wait()

    def split_prior(row, carry):
        for at in range(0, KPREV, BLOCK):
            high, low = split(prior[row, pl.ds(at, BLOCK), :])
            parts[row, pl.ds(at, BLOCK), :] = high
            parts[row, pl.ds(BOTH + at, BLOCK), :] = low
        return carry

    lax.fori_loop(0, ROWS, split_prior, 0)
    outs = [
        pltpu.make_async_copy(parts.at[row], split_out.at[row], out_sems.at[row]) for row in range(ROWS)
    ]
    for copy in outs:
        copy.start()
    total[...] = jnp.zeros_like(total)

    def products(row, carry):
        block = parts[row]
        total[...] += lax.dot_general(
            block, block, (((1,), (1,)), ((), ())), preferred_element_type=jnp.float32
        )
        return carry

    lax.fori_loop(0, ROWS, products, 0)
    inner = (
        total[0:BOTH, 0:BOTH] + (total[BOTH:, 0:BOTH] + total[0:BOTH, BOTH:]) + total[BOTH:, BOTH:]
    )
    inner_out[0:KPREV] = inner[0:KPREV]
    new = inner[KPREV:, KPREV:]
    inner_out[KPREV:] = jnp.concatenate([new[: KPREV // 2], new[KPREV // 2 :]], axis=1)
    for copy in outs:
        copy.wait()


def finish_kernel(inner, split_in, basis_out, triangle_out, parts, result, in_sems, out_sems):
    loads = [
        pltpu.make_async_copy(split_in.at[row], parts.at[row], in_sems.at[row]) for row in range(ROWS)
    ]
    for copy in loads:
        copy.start()

    def dot(a, b, dims):
        return lax.dot_general(
            a, b, (dims, ((), ())), precision=lax.Precision.HIGHEST, preferred_element_type=jnp.float32
        )

    prior = inner[0:KPREV, 0:KPREV]
    coeffs = inner[0:KPREV, KPREV:]
    half = KPREV // 2
    new = jnp.concatenate([inner[KPREV:, 0:KPREV], inner[KPREV:, KPREV:]], axis=0)
    mixed = dot(prior, coeffs, ((1,), (0,))) - 2.0 * coeffs
    gram = new + dot(coeffs, mixed, ((0,), (0,)))
    del half
    row_id = lax.broadcasted_iota(jnp.int32, (KPREV, 2 * KPREV), 0)
    col_id = lax.broadcasted_iota(jnp.int32, (KPREV, 2 * KPREV), 1)
    unit = jnp.where(
        lax.broadcasted_iota(jnp.int32, (KPREV, KPREV), 0)
        == lax.broadcasted_iota(jnp.int32, (KPREV, KPREV), 1),
        1.0,
        0.0,
    )
    work = jnp.concatenate([gram, unit], axis=1)
    for pivot in range(KPREV - 1):
        row = work[pivot : pivot + 1, :]
        scaled = row * (1.0 / row[:, pivot : pivot + 1])
        column = work[:, pivot : pivot + 1]
        work = jnp.where(row_id > pivot, work - column * scaled, work)
    diagonal = jnp.sum(jnp.where(row_id == col_id, work, 0.0), axis=1, keepdims=True)
    work = work / jnp.sqrt(diagonal)
    upper = work[:, :KPREV]
    triangle_out[...] = jnp.where(col_id[:, :KPREV] >= row_id[:, :KPREV], upper, 0.0)
    unknowns = 2 * 4 * 512 * 1024
    inverse = work[:, KPREV:] * math.sqrt(unknowns)
    weights = jnp.concatenate([-dot(inverse, coeffs, ((1,), (1,))), inverse], axis=1)
    high, low = split(weights)
    left = jnp.concatenate(
        [
            jnp.concatenate([high, high], axis=1),
            jnp.concatenate([low, jnp.zeros_like(low)], axis=1),
        ],
        axis=0,
    )
    stores = []
    for row in range(ROWS):
        loads[row].wait()
        for comp in range(COMPS):
            both = jnp.dot(
                left, parts[row, :, comp * COLS : (comp + 1) * COLS], preferred_element_type=jnp.float32
            )
            result[row, comp] = both[:KPREV] + both[KPREV:]
            copy = pltpu.make_async_copy(
                result.at[row, comp], basis_out.at[:, comp, row, :], out_sems.at[row, comp]
            )
            copy.start()
            stores.append(copy)
    for copy in stores:
        copy.wait()


def pairs_in(size, partner):
    return [(i, partner(i)) for i in range(size) if partner(i) is not None]


def row_exchange(value, bands, across):
    def partner(i):
        j = i + (1 if (i % 2 == 0) == (not across) else -1)
        return j if 0 <= j < bands else None

    return lax.ppermute(value, "band", pairs_in(bands, partner))


def col_exchange(value, cols, odd):
    def partner(i):
        j = i + (1 if (i % 2 == 0) == (not odd) else -1)
        return j if 0 <= j < cols else None

    return lax.ppermute(value, "col", pairs_in(cols, partner))


def sum_over_devices(value, bands, cols):
    def swap(part, mask):
        bits = cols - 1
        col_mask, band_mask = mask & bits, mask // cols
        perm = [(i, i ^ mask) for i in range(bands * cols)]
        del col_mask, band_mask
        return lax.ppermute(part, ("band", "col"), perm)

    mask = 1
    masks = []
    while mask < bands * cols:
        masks.append(mask)
        mask *= 2
    masks.sort(key=lambda m: (m != cols, m))
    for mask in masks:
        value = value + swap(value, mask)
    return value


def per_device(prior_basis, coupling, velocity):
    bands, cols = lax.axis_size("band"), lax.axis_size("col")
    f32 = jnp.float32
    basis = prior_basis.reshape(KPREV, COMPS, ROWS, COLS)
    slab, to_core, to_chip, edges = pl.pallas_call(
        pack_kernel,
        out_shape=(
            jax.ShapeDtypeStruct((ROWS, SLAB, COLS), f32),
            jax.ShapeDtypeStruct((WIDTH, SLAB, COLS), f32),
            jax.ShapeDtypeStruct((WIDTH, SLAB, COLS), f32),
            jax.ShapeDtypeStruct((PACKED, 8, LANES), f32),
        ),
        in_specs=[ANY, ANY, VMEM],
        out_specs=(ANY, ANY, ANY, VMEM),
        scratch_shapes=[
            pltpu.VMEM((ROWS, SLAB, COLS), f32),
            pltpu.SemaphoreType.DMA((ROWS, COMPS + 1)),
            pltpu.SemaphoreType.DMA((3,)),
        ],
        name="pack",
    )(basis, coupling.reshape(COUPLINGS, ROWS, COLS), velocity)
    side_even = col_exchange(edges, cols, False)
    side_odd = col_exchange(edges, cols, True)
    from_core = row_exchange(to_core, bands, False)
    from_chip = row_exchange(to_chip, bands, True)
    col_is_even = lax.rem(lax.axis_index("col"), 2) == 0
    from_right = lax.broadcasted_iota(jnp.int32, edges.shape, 2) % 8 >= 4
    sides = jnp.where(from_right == col_is_even, side_even, side_odd)
    core_sides = row_exchange(sides, bands, False)
    chip_sides = row_exchange(sides, bands, True)
    parts, inner = pl.pallas_call(
        power_kernel,
        out_shape=(
            jax.ShapeDtypeStruct((ROWS, 2 * BOTH, COMPS * COLS), jnp.bfloat16),
            jax.ShapeDtypeStruct((KPREV + KPREV // 2, BOTH), f32),
        ),
        in_specs=[ANY, ANY, ANY, ANY, VMEM, VMEM, VMEM],
        out_specs=(ANY, VMEM),
        scratch_shapes=[
            pltpu.VMEM((SPAN, PLANES, WIDE), f32),
            pltpu.VMEM((SPAN, PLANES, WIDE), f32),
            pltpu.VMEM((SPAN, COEFFS, WIDE), f32),
            pltpu.VMEM((ROWS, KPREV, COMPS * COLS), f32),
            pltpu.VMEM((ROWS, 2 * BOTH, COMPS * COLS), jnp.bfloat16),
            pltpu.VMEM((2 * BOTH, 2 * BOTH), f32),
            pltpu.SemaphoreType.DMA((ROWS, COMPS)),
            pltpu.SemaphoreType.DMA((6,)),
            pltpu.SemaphoreType.DMA((ROWS,)),
        ],
        compiler_params=pltpu.CompilerParams(vmem_limit_bytes=48 * 1024 * 1024),
        name="powers",
    )(basis, slab, from_core, from_chip, sides, core_sides, chip_sides)
    inner = sum_over_devices(inner, bands, cols)
    basis_next, triangle = pl.pallas_call(
        finish_kernel,
        out_shape=(
            jax.ShapeDtypeStruct((KPREV, COMPS, ROWS, COLS), f32),
            jax.ShapeDtypeStruct((KPREV, KPREV), f32),
        ),
        in_specs=[VMEM, ANY],
        out_specs=(ANY, VMEM),
        scratch_shapes=[
            pltpu.VMEM((ROWS, 2 * BOTH, COMPS * COLS), jnp.bfloat16),
            pltpu.VMEM((ROWS, COMPS, KPREV, COLS), f32),
            pltpu.SemaphoreType.DMA((ROWS,)),
            pltpu.SemaphoreType.DMA((ROWS, COMPS)),
        ],
        compiler_params=pltpu.CompilerParams(vmem_limit_bytes=48 * 1024 * 1024),
        name="finish",
    )(inner, parts)
    return (basis_next.reshape(prior_basis.shape), triangle)


def solution(mesh):
    in_specs = (
        P(None, None, None, "band", "col"),
        P(None, None, None, "band", "col"),
        P(None, "band", "col"),
    )
    out_specs = (P(None, None, None, "band", "col"), P())
    return jax.shard_map(
        per_device, mesh=mesh, in_specs=in_specs, out_specs=out_specs, check_vma=False
    )
```

profile of v0, /device:TPU:2, one launch (start us, length us, event | category | flops | bytes accessed | tf_op | source)
XLA Modules:
  0.0 106.7 jit_solution(5545220620918565534)
XLA Ops:
  0.6 5.1 %pack.1 = (f32[8,168,256]{2,1,0:T(8,128)}, f32[4,168,256]{2,1,0:T(8,128)}, f32[4,168,256]{2,1,0:T(8,128)}, f32[11,8,128]{2,1,0:T(8,128)}) custom-call(f32[64,8,8,256]{3,2,1,0:T(8,128)} %bitcast.3, f32[32,8,256]{2,1,0:T(8,128)} %bitcast.5, f32[2,8,256]{2,1,0:T(8,128)} %velocity.1), custom_call_target="tpu_custom_call" | custom-call | tf_op jit(solution)/shard_map/pack/pallas_call | solution.py:368
  5.8 0.1 collective-permute-start
  5.9 0.7 collective-permute-start.1
  6.6 3.4 %collective-permute-start.3 = (f32[11,8,128]{2,1,0:T(8,128)}, f32[11,8,128]{2,1,0:T(8,128)S(1)}, u32[]{:S(2)}, u32[]{:S(2)}) collective-permute-start(f32[11,8,128]{2,1,0:T(8,128)} %get-tuple-element.13), channel_id=1, source_target_pairs={{1,2},{2,1},{5,6},{6,5},{9,10},{10,9},{13,14},{14,13},{17,18},{18,... | collective-permute-start | bytes 135176 | tf_op jit(solution)/shard_map/ppermute | solution.py:342
  10.0 0.1 collective-permute-start.2
  10.1 2.6 %collective-permute-done.3 = f32[11,8,128]{2,1,0:T(8,128)S(1)} collective-permute-done((f32[11,8,128]{2,1,0:T(8,128)}, f32[11,8,128]{2,1,0:T(8,128)S(1)}, u32[]{:S(2)}, u32[]{:S(2)}) %collective-permute-start.3) | collective-permute-done | bytes 45088 | tf_op jit(solution)/shard_map/ppermute | solution.py:342
  12.7 1.6 %collective-permute-done.2 = f32[11,8,128]{2,1,0:T(8,128)S(1)} collective-permute-done((f32[11,8,128]{2,1,0:T(8,128)}, f32[11,8,128]{2,1,0:T(8,128)S(1)}, u32[]{:S(2)}, u32[]{:S(2)}) %collective-permute-start.2) | collective-permute-done | bytes 45088 | tf_op jit(solution)/shard_map/ppermute | solution.py:342
  14.3 0.7 collective-permute-start.5
  15.0 5.2 %collective-permute-start.4 = (f32[11,8,128]{2,1,0:T(8,128)S(1)}, f32[11,8,128]{2,1,0:T(8,128)S(1)}, u32[]{:S(2)}, u32[]{:S(2)}) collective-permute-start(f32[11,8,128]{2,1,0:T(8,128)S(1)} %fusion.1.sides), channel_id=1, source_target_pairs={{0,4},{4,0},{8,12},{12,8},{16,20},{20,16},{24,28},{28,24},{32,36},... | collective-permute-start | bytes 135176 | tf_op jit(solution)/shard_map/ppermute | solution.py:334
  20.2 0.0 collective-permute-done.5.chip_sides
  20.2 0.9 collective-permute-done.4.core_sides
  21.0 0.0 collective-permute-done.from_core
  21.1 0.0 collective-permute-done.1.from_chip
  21.1 0.0 copy-start
  21.1 1.3 %copy-done = f32[8,168,256]{2,1,0:T(8,128)S(1)} copy-done((f32[8,168,256]{2,1,0:T(8,128)S(1)}, f32[8,168,256]{2,1,0:T(8,128)}, u32[]{:S(2)}) %copy-start) | copy-done | bytes 1376280
  22.4 17.7 %powers.1 = (bf16[8,256,2048]{2,1,0:T(8,128)(2,1)}, f32[96,128]{1,0:T(8,128)S(1)}) custom-call(f32[64,8,8,256]{3,2,1,0:T(8,128)} %bitcast.4, f32[8,168,256]{2,1,0:T(8,128)S(1)} %copy-done, f32[4,168,256]{2,1,0:T(8,128)S(1)} %collective-permute-done.from_core, f32[4,168,256]{2,1,0:T(8,128)S(1)} %collective-permute-done.1.from_chip, ...), custom_call_target="tpu_custom_call" | custom-call | tf_op jit(solution)/shard_map/powers/pallas_call | solution.py:394
  40.1 0.8 collective-permute-start.6
  41.0 0.9 collective-permute-done.6
  41.9 0.0 collective-permute-start.7
  41.9 4.1 %collective-permute-done.7 = f32[96,128]{1,0:T(8,128)S(1)} collective-permute-done((f32[96,128]{1,0:T(8,128)S(1)}, f32[96,128]{1,0:T(8,128)S(1)}, u32[]{:S(2)}, u32[]{:S(2)}) %collective-permute-start.7) | collective-permute-done | bytes 49184 | tf_op jit(solution)/shard_map/ppermute | solution.py:351
  46.0 0.3 collective-permute-start.8
  46.3 5.3 %collective-permute-done.8 = f32[96,128]{1,0:T(8,128)S(1)} collective-permute-done((f32[96,128]{1,0:T(8,128)S(1)}, f32[96,128]{1,0:T(8,128)S(1)}, u32[]{:S(2)}, u32[]{:S(2)}) %collective-permute-start.8) | collective-permute-done | bytes 49184 | tf_op jit(solution)/shard_map/ppermute | solution.py:351
  51.6 2.1 %collective-permute-start.9 = (f32[96,128]{1,0:T(8,128)S(1)}, f32[96,128]{1,0:T(8,128)S(1)}, u32[]{:S(2)}, u32[]{:S(2)}) collective-permute-start(f32[96,128]{1,0:T(8,128)S(1)} %add.34), channel_id=1, source_target_pairs={{0,8},{1,9},{2,10},{3,11},{4,12},{5,13},{6,14},{7,15},{8,0},{9,1},... | collective-permute-start | bytes 147464 | tf_op jit(solution)/shard_map/ppermute | solution.py:351
  53.8 2.1 %collective-permute-done.9 = f32[96,128]{1,0:T(8,128)S(1)} collective-permute-done((f32[96,128]{1,0:T(8,128)S(1)}, f32[96,128]{1,0:T(8,128)S(1)}, u32[]{:S(2)}, u32[]{:S(2)}) %collective-permute-start.9) | collective-permute-done | bytes 49184 | tf_op jit(solution)/shard_map/ppermute | solution.py:351
  55.8 4.6 %collective-permute-start.10 = (f32[96,128]{1,0:T(8,128)S(1)}, f32[96,128]{1,0:T(8,128)S(1)}, u32[]{:S(2)}, u32[]{:S(2)}) collective-permute-start(f32[96,128]{1,0:T(8,128)S(1)} %add.35), channel_id=1, source_target_pairs={{0,16},{1,17},{2,18},{3,19},{4,20},{5,21},{6,22},{7,23},{8,24},{9,... | collective-permute-start | bytes 147464 | tf_op jit(solution)/shard_map/ppermute | solution.py:351
  60.4 2.1 %collective-permute-done.10 = f32[96,128]{1,0:T(8,128)S(1)} collective-permute-done((f32[96,128]{1,0:T(8,128)S(1)}, f32[96,128]{1,0:T(8,128)S(1)}, u32[]{:S(2)}, u32[]{:S(2)}) %collective-permute-start.10) | collective-permute-done | bytes 49184 | tf_op jit(solution)/shard_map/ppermute | solution.py:351
  62.5 5.5 %collective-permute-start.11 = (f32[96,128]{1,0:T(8,128)S(1)}, f32[96,128]{1,0:T(8,128)S(1)}, u32[]{:S(2)}, u32[]{:S(2)}) collective-permute-start(f32[96,128]{1,0:T(8,128)S(1)} %add.36), channel_id=1, source_target_pairs={{0,32},{1,33},{2,34},{3,35},{4,36},{5,37},{6,38},{7,39},{8,40},{9,... | collective-permute-start | bytes 147464 | tf_op jit(solution)/shard_map/ppermute | solution.py:351
  68.0 2.1 %collective-permute-done.11 = f32[96,128]{1,0:T(8,128)S(1)} collective-permute-done((f32[96,128]{1,0:T(8,128)S(1)}, f32[96,128]{1,0:T(8,128)S(1)}, u32[]{:S(2)}, u32[]{:S(2)}) %collective-permute-start.11) | collective-permute-done | bytes 49184 | tf_op jit(solution)/shard_map/ppermute | solution.py:351
  70.1 3.5 %collective-permute-start.12 = (f32[96,128]{1,0:T(8,128)S(1)}, f32[96,128]{1,0:T(8,128)S(1)}, u32[]{:S(2)}, u32[]{:S(2)}) collective-permute-start(f32[96,128]{1,0:T(8,128)S(1)} %add.37), channel_id=1, source_target_pairs={{0,64},{1,65},{2,66},{3,67},{4,68},{5,69},{6,70},{7,71},{8,72},{9,... | collective-permute-start | bytes 147464 | tf_op jit(solution)/shard_map/ppermute | solution.py:351
  73.6 2.1 %collective-permute-done.12 = f32[96,128]{1,0:T(8,128)S(1)} collective-permute-done((f32[96,128]{1,0:T(8,128)S(1)}, f32[96,128]{1,0:T(8,128)S(1)}, u32[]{:S(2)}, u32[]{:S(2)}) %collective-permute-start.12) | collective-permute-done | bytes 49184 | tf_op jit(solution)/shard_map/ppermute | solution.py:351
  75.7 9.1 %collective-permute-start.13 = (f32[96,128]{1,0:T(8,128)S(1)}, f32[96,128]{1,0:T(8,128)S(1)}, u32[]{:S(2)}, u32[]{:S(2)}) collective-permute-start(f32[96,128]{1,0:T(8,128)S(1)} %add.38), channel_id=1, source_target_pairs={{0,128},{1,129},{2,130},{3,131},{4,132},{5,133},{6,134},{7,135},{8... | collective-permute-start | bytes 147464 | tf_op jit(solution)/shard_map/ppermute | solution.py:351
  84.8 2.1 %collective-permute-done.13 = f32[96,128]{1,0:T(8,128)S(1)} collective-permute-done((f32[96,128]{1,0:T(8,128)S(1)}, f32[96,128]{1,0:T(8,128)S(1)}, u32[]{:S(2)}, u32[]{:S(2)}) %collective-permute-start.13) | collective-permute-done | bytes 49184 | tf_op jit(solution)/shard_map/ppermute | solution.py:351
  86.9 19.7 %finish.1 = (f32[64,8,8,256]{3,2,1,0:T(8,128)}, f32[64,64]{1,0:T(8,128)}) custom-call(f32[96,128]{1,0:T(8,128)S(1)} %add.39.inner, bf16[8,256,2048]{2,1,0:T(8,128)(2,1)} %get-tuple-element.15.split_in), custom_call_target="tpu_custom_call" | custom-call | tf_op jit(solution)/shard_map/finish/pallas_call | solution.py:417
  (11 shorter events, 0.1 us)
Async XLA Ops:
  5.8 15.3 %collective-permute-start = (f32[4,168,256]{2,1,0:T(8,128)}, f32[4,168,256]{2,1,0:T(8,128)S(1)}, u32[]{:S(2)}, u32[]{:S(2)}) collective-permute-start(f32[4,168,256]{2,1,0:T(8,128)} %get-tuple-element.11), channel_id=1, source_target_pairs={{0,4},{4,0},{8,12},{12,8},{16,20},{20,16},{24,28},{28,24},{32,36},... | collective-permute-start | bytes 2064392 | tf_op jit(solution)/shard_map/ppermute | solution.py:334
  5.9 15.2 %collective-permute-start.1 = (f32[4,168,256]{2,1,0:T(8,128)}, f32[4,168,256]{2,1,0:T(8,128)S(1)}, u32[]{:S(2)}, u32[]{:S(2)}) collective-permute-start(f32[4,168,256]{2,1,0:T(8,128)} %get-tuple-element.12), channel_id=1, source_target_pairs={{4,8},{8,4},{12,16},{16,12},{20,24},{24,20},{28,32},{32,28},{36,40... | collective-permute-start | bytes 2064392 | tf_op jit(solution)/shard_map/ppermute | solution.py:334
  6.6 6.2 %collective-permute-start.3 = (f32[11,8,128]{2,1,0:T(8,128)}, f32[11,8,128]{2,1,0:T(8,128)S(1)}, u32[]{:S(2)}, u32[]{:S(2)}) collective-permute-start(f32[11,8,128]{2,1,0:T(8,128)} %get-tuple-element.13), channel_id=1, source_target_pairs={{1,2},{2,1},{5,6},{6,5},{9,10},{10,9},{13,14},{14,13},{17,18},{18,... | collective-permute-start | bytes 135176 | tf_op jit(solution)/shard_map/ppermute | solution.py:342
  10.0 4.3 %collective-permute-start.2 = (f32[11,8,128]{2,1,0:T(8,128)}, f32[11,8,128]{2,1,0:T(8,128)S(1)}, u32[]{:S(2)}, u32[]{:S(2)}) collective-permute-start(f32[11,8,128]{2,1,0:T(8,128)} %get-tuple-element.13), channel_id=1, source_target_pairs={{0,1},{1,0},{2,3},{3,2},{4,5},{5,4},{6,7},{7,6},{8,9},{9,8},{10,11... | collective-permute-start | bytes 135176 | tf_op jit(solution)/shard_map/ppermute | solution.py:342
  14.3 5.8 %collective-permute-start.5 = (f32[11,8,128]{2,1,0:T(8,128)S(1)}, f32[11,8,128]{2,1,0:T(8,128)S(1)}, u32[]{:S(2)}, u32[]{:S(2)}) collective-permute-start(f32[11,8,128]{2,1,0:T(8,128)S(1)} %fusion.1.sides), channel_id=1, source_target_pairs={{4,8},{8,4},{12,16},{16,12},{20,24},{24,20},{28,32},{32,28},{36,40... | collective-permute-start | bytes 135176 | tf_op jit(solution)/shard_map/ppermute | solution.py:334
  15.0 6.0 %collective-permute-start.4 = (f32[11,8,128]{2,1,0:T(8,128)S(1)}, f32[11,8,128]{2,1,0:T(8,128)S(1)}, u32[]{:S(2)}, u32[]{:S(2)}) collective-permute-start(f32[11,8,128]{2,1,0:T(8,128)S(1)} %fusion.1.sides), channel_id=1, source_target_pairs={{0,4},{4,0},{8,12},{12,8},{16,20},{20,16},{24,28},{28,24},{32,36},... | collective-permute-start | bytes 135176 | tf_op jit(solution)/shard_map/ppermute | solution.py:334
  21.1 1.3 %copy-start = (f32[8,168,256]{2,1,0:T(8,128)S(1)}, f32[8,168,256]{2,1,0:T(8,128)}, u32[]{:S(2)}) copy-start(f32[8,168,256]{2,1,0:T(8,128)} %get-tuple-element.10.slab) | copy-start | bytes 4128772
  40.1 1.7 %collective-permute-start.6 = (f32[96,128]{1,0:T(8,128)S(1)}, f32[96,128]{1,0:T(8,128)S(1)}, u32[]{:S(2)}, u32[]{:S(2)}) collective-permute-start(f32[96,128]{1,0:T(8,128)S(1)} %get-tuple-element.14), channel_id=1, source_target_pairs={{0,4},{1,5},{2,6},{3,7},{4,0},{5,1},{6,2},{7,3},{8,12},{9,13},{10,... | collective-permute-start | bytes 147464 | tf_op jit(solution)/shard_map/ppermute | solution.py:351
  41.9 4.1 %collective-permute-start.7 = (f32[96,128]{1,0:T(8,128)S(1)}, f32[96,128]{1,0:T(8,128)S(1)}, u32[]{:S(2)}, u32[]{:S(2)}) collective-permute-start(f32[96,128]{1,0:T(8,128)S(1)} %add.32), channel_id=1, source_target_pairs={{0,1},{1,0},{2,3},{3,2},{4,5},{5,4},{6,7},{7,6},{8,9},{9,8},{10,11... | collective-permute-start | bytes 147464 | tf_op jit(solution)/shard_map/ppermute | solution.py:351
  46.0 5.7 %collective-permute-start.8 = (f32[96,128]{1,0:T(8,128)S(1)}, f32[96,128]{1,0:T(8,128)S(1)}, u32[]{:S(2)}, u32[]{:S(2)}) collective-permute-start(f32[96,128]{1,0:T(8,128)S(1)} %add.33), channel_id=1, source_target_pairs={{0,2},{1,3},{2,0},{3,1},{4,6},{5,7},{6,4},{7,5},{8,10},{9,11},{10,... | collective-permute-start | bytes 147464 | tf_op jit(solution)/shard_map/ppermute | solution.py:351
  51.6 4.2 %collective-permute-start.9 = (f32[96,128]{1,0:T(8,128)S(1)}, f32[96,128]{1,0:T(8,128)S(1)}, u32[]{:S(2)}, u32[]{:S(2)}) collective-permute-start(f32[96,128]{1,0:T(8,128)S(1)} %add.34), channel_id=1, source_target_pairs={{0,8},{1,9},{2,10},{3,11},{4,12},{5,13},{6,14},{7,15},{8,0},{9,1},... | collective-permute-start | bytes 147464 | tf_op jit(solution)/shard_map/ppermute | solution.py:351
  55.8 6.7 %collective-permute-start.10 = (f32[96,128]{1,0:T(8,128)S(1)}, f32[96,128]{1,0:T(8,128)S(1)}, u32[]{:S(2)}, u32[]{:S(2)}) collective-permute-start(f32[96,128]{1,0:T(8,128)S(1)} %add.35), channel_id=1, source_target_pairs={{0,16},{1,17},{2,18},{3,19},{4,20},{5,21},{6,22},{7,23},{8,24},{9,... | collective-permute-start | bytes 147464 | tf_op jit(solution)/shard_map/ppermute | solution.py:351
  62.5 7.6 %collective-permute-start.11 = (f32[96,128]{1,0:T(8,128)S(1)}, f32[96,128]{1,0:T(8,128)S(1)}, u32[]{:S(2)}, u32[]{:S(2)}) collective-permute-start(f32[96,128]{1,0:T(8,128)S(1)} %add.36), channel_id=1, source_target_pairs={{0,32},{1,33},{2,34},{3,35},{4,36},{5,37},{6,38},{7,39},{8,40},{9,... | collective-permute-start | bytes 147464 | tf_op jit(solution)/shard_map/ppermute | solution.py:351
  70.1 5.5 %collective-permute-start.12 = (f32[96,128]{1,0:T(8,128)S(1)}, f32[96,128]{1,0:T(8,128)S(1)}, u32[]{:S(2)}, u32[]{:S(2)}) collective-permute-start(f32[96,128]{1,0:T(8,128)S(1)} %add.37), channel_id=1, source_target_pairs={{0,64},{1,65},{2,66},{3,67},{4,68},{5,69},{6,70},{7,71},{8,72},{9,... | collective-permute-start | bytes 147464 | tf_op jit(solution)/shard_map/ppermute | solution.py:351
  75.7 11.2 %collective-permute-start.13 = (f32[96,128]{1,0:T(8,128)S(1)}, f32[96,128]{1,0:T(8,128)S(1)}, u32[]{:S(2)}, u32[]{:S(2)}) collective-permute-start(f32[96,128]{1,0:T(8,128)S(1)} %add.38), channel_id=1, source_target_pairs={{0,128},{1,129},{2,130},{3,131},{4,132},{5,133},{6,134},{7,135},{8... | collective-permute-start | bytes 147464 | tf_op jit(solution)/shard_map/ppermute | solution.py:351
where the time goes:
time: 107 us
  Pallas kernels  42.5 us (40%)
  starting transfers between devices  36.1 us (34%)
  waiting for transfers between devices  25.8 us (24%)
  local copies, waits for them, and re-layouts  1.34 us (1%)
    ppermute x8, starting transfers between devices, swap(): return lax.ppermute(part, ('band', 'col'), perm)  26 us
    ppermute x8, waiting for transfers between devices, swap(): return lax.ppermute(part, ('band', 'col'), perm)  20.7 us
    pallas_call x1, Pallas kernels, per_device(): pl.pallas_call(finish_kernel, out_shape=(jax.ShapeDtypeStruct((KPREV, COM...  19.7 us
    pallas_call x1, Pallas kernels, per_device(): pl.pallas_call(power_kernel, out_shape=(jax.ShapeDtypeStruct((ROWS, 2 * B...  17.7 us
    ppermute x4, starting transfers between devices, row_exchange(): return lax.ppermute(value, 'band', pairs_in(bands, partner))  6.61 us
    pallas_call x1, Pallas kernels, per_device(): pl.pallas_call(pack_kernel, out_shape=(jax.ShapeDtypeStruct((ROWS, SLAB,...  5.14 us
    ppermute x2, waiting for transfers between devices, col_exchange(): return lax.ppermute(value, 'col', pairs_in(cols, partner))  4.22 us
    ppermute x2, starting transfers between devices, col_exchange(): return lax.ppermute(value, 'col', pairs_in(cols, partner))  3.49 us
  transfers between devices with their start and end apart: 14, of which 11 were waited for; matrix products, arithmetic and copies ran while one was open for 0% of the time, Pallas kernels for 0%

commit v1 on v0

v1 whole, which is shorter than its diff:
```python
import math

import jax
import jax.numpy as jnp
from jax import lax
from jax.experimental import pallas as pl
from jax.experimental.pallas import tpu as pltpu
from jax.sharding import PartitionSpec as P

BLOCK = 16
STEPS = 4
KPREV = 64
COMPS = 8
ROWS = 8
COLS = 256
LANES = 128
WIDTH = 4
PLANES = COMPS * BLOCK
COUPLINGS = 32
COEFFS = 40
SLAB = PLANES + COEFFS
TILES = SLAB // 8
PACKED = (TILES + 1) // 2
SPAN = ROWS + 2 * WIDTH
WIDE = COLS + LANES
BOTH = 2 * KPREV
PIVOTS = 8
CELL_ROWS = COMPS * ROWS
OUT = pltpu.VMEM

ANY = pl.BlockSpec(memory_space=pl.ANY)
VMEM = pl.BlockSpec(memory_space=pltpu.VMEM)
HBM = pl.BlockSpec(memory_space=pltpu.HBM)


def core_of_chip():
    return lax.rem(lax.axis_index("band"), 2)


def pack_kernel(basis, coupling, velocity, slab, core_out, chip_out, edges, start, mixing, sems):
    loads = []
    for half in range(2):
        lanes = pl.ds(half * LANES, LANES)
        loads += [
            pltpu.make_async_copy(
                basis.at[pl.ds((KPREV - BLOCK) * CELL_ROWS, BLOCK * CELL_ROWS), lanes],
                start.at[half],
                sems.at[half],
            ),
            pltpu.make_async_copy(coupling.at[:, lanes], mixing.at[half], sems.at[2 + half]),
        ]
    for copy in loads:
        copy.start()
    half_rows = 0.5 * velocity[0]
    half_cols = 0.5 * velocity[1]
    stencil = (0.15 - half_rows, 0.15 + half_rows, 0.15 - half_cols, 0.15 + half_cols)
    blank = jnp.zeros((4, COLS), jnp.float32)
    for row in range(ROWS):
        slab[row, PLANES + COUPLINGS :, :] = jnp.concatenate(
            [part[row : row + 1] for part in stencil] + [blank], axis=0
        )
    for copy in loads:
        copy.wait()
    for row in range(ROWS):
        for half in range(2):
            lanes = slice(half * LANES, (half + 1) * LANES)
            for comp in range(COMPS):
                slab[row, comp * BLOCK : (comp + 1) * BLOCK, lanes] = start[
                    half, pl.ds(comp * ROWS + row, BLOCK, stride=CELL_ROWS), :
                ]
            slab[row, PLANES : PLANES + COUPLINGS, lanes] = mixing[
                half, pl.ds(row, COUPLINGS, stride=ROWS), :
            ]
    core = core_of_chip()
    for row in range(WIDTH):
        core_out[row] = slab[row + (1 - core) * WIDTH]
        chip_out[row] = slab[row + core * WIDTH]
    lane = lax.broadcasted_iota(jnp.int32, (8, LANES), 1)
    for packed in range(PACKED):
        total = jnp.zeros((8, LANES), jnp.float32)
        for half in range(2):
            tile = 2 * packed + half
            if tile >= TILES:
                continue
            for row in range(ROWS):
                group = half * ROWS + row
                first = slab[row, tile * 8 : tile * 8 + 8, 0:LANES]
                last = slab[row, tile * 8 : tile * 8 + 8, COLS - LANES : COLS]
                edge = pltpu.roll(jnp.where(lane < WIDTH, first, last), (8 * group + 4) % LANES, 1)
                total = jnp.where(lane // 8 == group, edge, total)
        edges[packed] = total


def split(value):
    high = value.astype(jnp.bfloat16)
    return high, (value - high.astype(jnp.float32)).astype(jnp.bfloat16)


def prior_kernel(basis, parts, token, native, sems):
    pieces = KPREV // BLOCK
    size = BLOCK * CELL_ROWS
    loads = [
        pltpu.make_async_copy(
            basis.at[pl.ds(piece * size, size), pl.ds(half * LANES, LANES)],
            native.at[half, pl.ds(piece * size, size), :],
            sems.at[piece, half],
        )
        for piece in range(pieces)
        for half in range(2)
    ]
    for copy in loads:
        copy.start()
    for piece in range(pieces):
        loads[2 * piece].wait()
        loads[2 * piece + 1].wait()

        def one_row(row, carry, piece=piece):
            for comp in range(COMPS):
                for half in range(2):
                    at = piece * size + comp * ROWS
                    high, low = split(native[half, pl.ds(at + row, BLOCK, stride=CELL_ROWS), :])
                    cells = pl.ds(comp * COLS + half * LANES, LANES)
                    parts[row, pl.ds(piece * BLOCK, BLOCK), cells] = high
                    parts[row, pl.ds(KPREV + piece * BLOCK, BLOCK), cells] = low
            return carry

        lax.fori_loop(0, ROWS, one_row, 0)
    token[...] = jnp.zeros_like(token)


def merge_kernel(side_even, side_odd, after, sides):
    del after
    col_is_even = lax.rem(lax.axis_index("col"), 2) == 0
    from_right = lax.broadcasted_iota(jnp.int32, side_even.shape, 2) % 8 >= 4
    sides[...] = jnp.where(from_right == col_is_even, side_even[...], side_odd[...])


def dot_rows(a, b):
    return lax.dot_general(a, b, (((1,), (1,)), ((), ())), preferred_element_type=jnp.float32)


def join_parts(total):
    crossed = total[KPREV:, 0:KPREV] + total[0:KPREV, KPREV:]
    return total[0:KPREV, 0:KPREV] + crossed + total[KPREV:, KPREV:]


def operator_row(cur, nxt, coef, row, tiles):
    lane = lax.broadcasted_iota(jnp.int32, (BLOCK, LANES), 1)
    is_first, is_last = lane == 0, lane == LANES - 1
    for tile in range(tiles):
        lanes, after, before = (
            pl.ds((tile + shift) % (WIDE // LANES) * LANES, LANES) for shift in (0, 1, WIDE // LANES - 1)
        )

        def coeff(plane, lanes=lanes):
            return jnp.broadcast_to(coef[row, pl.ds(plane, 1), lanes], (BLOCK, LANES))

        def neighbours(comp, here, lanes=lanes, after=after, before=before, coeff=coeff):
            planes = pl.ds(comp * BLOCK, BLOCK)
            right = pltpu.roll(jnp.where(is_first, cur[row, planes, after], here), LANES - 1, 1)
            left = pltpu.roll(jnp.where(is_last, cur[row, planes, before], here), 1, 1)
            return (
                coeff(COUPLINGS) * cur[row + 1, planes, lanes]
                + coeff(COUPLINGS + 1) * cur[row - 1, planes, lanes]
                + coeff(COUPLINGS + 2) * right
                + coeff(COUPLINGS + 3) * left
            )

        center = [cur[row, pl.ds(comp * BLOCK, BLOCK), lanes] for comp in range(COMPS)]
        for field in range(4):
            real = neighbours(field, center[field])
            imag = neighbours(4 + field, center[4 + field])
            for source in range(4):
                coeff_real = coeff(field * 4 + source)
                coeff_imag = coeff(16 + field * 4 + source)
                if source == field:
                    coeff_real = coeff_real - 0.6
                real = real + coeff_real * center[source] - coeff_imag * center[4 + source]
                imag = imag + coeff_real * center[4 + source] + coeff_imag * center[source]
            nxt[row, pl.ds(field * BLOCK, BLOCK), lanes] = real
            nxt[row, pl.ds((4 + field) * BLOCK, BLOCK), lanes] = imag


def power_kernel(
    slab, from_core, from_chip, sides, core_sides, chip_sides, prior_parts,
    parts, inner_out,
    ping, pong, coef, halo_sems,
):
    core = core_of_chip()
    is_first = core == 0
    core_at = pl.multiple_of((1 - core) * (SPAN - WIDTH), WIDTH)
    chip_at = pl.multiple_of(core * (SPAN - WIDTH), WIDTH)
    halos = []
    for index, (source, where, count) in enumerate(
        ((slab, WIDTH, ROWS), (from_core, core_at, WIDTH), (from_chip, chip_at, WIDTH))
    ):
        halos.append(
            pltpu.make_async_copy(
                source.at[:, pl.ds(0, PLANES), :],
                ping.at[pl.ds(where, count), :, pl.ds(0, COLS)],
                halo_sems.at[2 * index],
            )
        )
        halos.append(
            pltpu.make_async_copy(
                source.at[:, pl.ds(PLANES, COEFFS), :],
                coef.at[pl.ds(where, count), :, pl.ds(0, COLS)],
                halo_sems.at[2 * index + 1],
            )
        )
    for copy in halos:
        copy.start()
    lane = lax.broadcasted_iota(jnp.int32, (8, LANES), 1)
    near = (lane < WIDTH) | (lane >= LANES - WIDTH)
    for packed in range(PACKED):
        own = sides[packed]
        by_core, by_chip = core_sides[packed], chip_sides[packed]
        above = jnp.where(is_first, by_core, by_chip)
        below = jnp.where(is_first, by_chip, by_core)
        for half in range(2):
            tile = 2 * packed + half
            if tile >= TILES:
                continue
            for row in range(SPAN):
                if row < WIDTH:
                    source, source_row = below, row + ROWS - WIDTH
                elif row < WIDTH + ROWS:
                    source, source_row = own, row - WIDTH
                else:
                    source, source_row = above, row - WIDTH - ROWS
                group = half * ROWS + source_row
                edge = pltpu.roll(source, (2 * LANES - 8 * group - 4) % LANES, 1)
                edge = jnp.where(near, edge, 0.0)
                if tile < PLANES // 8:
                    ping[row, tile * 8 : tile * 8 + 8, COLS:WIDE] = edge
                else:
                    at = tile * 8 - PLANES
                    coef[row, at : at + 8, COLS:WIDE] = edge
    for copy in halos:
        copy.wait()
    buffers = (ping, pong)
    for step in range(1, STEPS + 1):
        cur, nxt = buffers[(step - 1) % 2], buffers[step % 2]
        tiles = 3 if step < STEPS else 2

        def one_row(row, carry, cur=cur, nxt=nxt, tiles=tiles):
            operator_row(cur, nxt, coef, row, tiles)
            return carry

        lax.fori_loop(step, SPAN - step, one_row, 0)

        def one_split(row, carry, nxt=nxt, step=step):
            at = (step - 1) * BLOCK
            for comp in range(COMPS):
                high, low = split(nxt[row + WIDTH, pl.ds(comp * BLOCK, BLOCK), 0:COLS])
                parts[row, pl.ds(at, BLOCK), pl.ds(comp * COLS, COLS)] = high
                parts[row, pl.ds(KPREV + at, BLOCK), pl.ds(comp * COLS, COLS)] = low
            return carry

        lax.fori_loop(0, ROWS, one_split, 0)
    total = 0.0
    for row in range(ROWS):
        block = jnp.concatenate([prior_parts[row], parts[row]], axis=0)
        total = total + dot_rows(block, block)
    inner_out[0:KPREV] = jnp.concatenate(
        [join_parts(total[:BOTH, :BOTH]), join_parts(total[:BOTH, BOTH:])], axis=1
    )
    new = join_parts(total[BOTH:, BOTH:])
    inner_out[KPREV:] = jnp.concatenate([new[: KPREV // 2], new[KPREV // 2 :]], axis=1)


def finish_kernel(inner, prior_parts, new_parts, basis_out, triangle_out, result, out_sems):
    def dot(a, b, dims):
        return lax.dot_general(
            a, b, (dims, ((), ())), precision=lax.Precision.HIGHEST, preferred_element_type=jnp.float32
        )

    prior = inner[0:KPREV, 0:KPREV]
    coeffs = inner[0:KPREV, KPREV:]
    new = jnp.concatenate([inner[KPREV:, 0:KPREV], inner[KPREV:, KPREV:]], axis=0)
    mixed = dot(prior, coeffs, ((1,), (0,))) - 2.0 * coeffs
    gram = new + dot(coeffs, mixed, ((0,), (0,)))
    col_id = lax.broadcasted_iota(jnp.int32, (KPREV, 2 * KPREV), 1)
    unit = jnp.where(
        lax.broadcasted_iota(jnp.int32, (KPREV, KPREV), 0)
        == lax.broadcasted_iota(jnp.int32, (KPREV, KPREV), 1),
        1.0,
        0.0,
    )
    work = jnp.concatenate([gram, unit], axis=1)
    done = []
    for pivot in range(0, KPREV, PIVOTS):
        top = pivot // 8 * 8
        if pivot % 8 == 0 and pivot:
            done.append(work[:8])
            work = work[8:]
        at = pivot - top
        row_id = lax.broadcasted_iota(jnp.int32, work.shape, 0)
        columns = [
            jnp.broadcast_to(work[:, pivot + i : pivot + i + 1], work.shape) for i in range(PIVOTS)
        ]
        rows = [work[at + i : at + i + 1] for i in range(PIVOTS)]
        for i in range(PIVOTS):
            column = columns[i]
            factor = jnp.where(row_id > at + i, column * (1.0 / column[at + i : at + i + 1]), 0.0)
            work = work - factor * rows[i]
            for j in range(i + 1, PIVOTS):
                rows[j] = rows[j] - factor[at + j : at + j + 1] * rows[i]
                columns[j] = columns[j] - factor * columns[j][at + i : at + i + 1]
    work = jnp.concatenate(done + [work], axis=0)
    row_id = lax.broadcasted_iota(jnp.int32, (KPREV, 2 * KPREV), 0)
    diagonal = jnp.sum(jnp.where(row_id == col_id, work, 0.0), axis=1, keepdims=True)
    work = work / jnp.sqrt(diagonal)
    upper = work[:, :KPREV]
    triangle_out[...] = jnp.where(col_id[:, :KPREV] >= row_id[:, :KPREV], upper, 0.0)
    unknowns = 2 * 4 * 512 * 1024
    inverse = work[:, KPREV:] * math.sqrt(unknowns)
    weights = jnp.concatenate(
        [two_parts(-dot(inverse, coeffs, ((1,), (1,)))), two_parts(inverse)], axis=1
    )
    rows = result.reshape(2, KPREV * CELL_ROWS, LANES)
    stores = []
    for comp in range(COMPS):
        cells = slice(comp * COLS, (comp + 1) * COLS)
        for row in range(ROWS):
            vectors = jnp.concatenate([prior_parts[row, :, cells], new_parts[row, :, cells]], axis=0)
            both = jnp.dot(weights, vectors, preferred_element_type=jnp.float32)
            both = both[:KPREV] + both[KPREV:]
            where = pl.ds(comp * ROWS + row, KPREV, stride=CELL_ROWS)
            for half in range(2):
                rows[half, where, :] = both[:, half * LANES : (half + 1) * LANES]
        for half in range(2):
            copy = pltpu.make_async_copy(
                result.at[half, :, comp],
                basis_out.at[:, comp, :, pl.ds(half * LANES, LANES)],
                out_sems.at[comp, half],
            )
            copy.start()
            stores.append(copy)
    for copy in stores:
        copy.wait()


def two_parts(weights):
    high, low = split(weights)
    return jnp.concatenate(
        [
            jnp.concatenate([high, high], axis=1),
            jnp.concatenate([low, jnp.zeros_like(low)], axis=1),
        ],
        axis=0,
    )


def pairs_in(size, partner):
    return [(i, partner(i)) for i in range(size) if partner(i) is not None]


def row_exchange(value, bands, across):
    def partner(i):
        j = i + (1 if (i % 2 == 0) == (not across) else -1)
        return j if 0 <= j < bands else None

    return lax.ppermute(value, "band", pairs_in(bands, partner))


def col_exchange(value, cols, odd):
    def partner(i):
        j = i + (1 if (i % 2 == 0) == (not odd) else -1)
        return j if 0 <= j < cols else None

    return lax.ppermute(value, "col", pairs_in(cols, partner))


def sum_over_devices(value, bands, cols):
    def from_partner(mask):
        return lax.ppermute(
            value, ("band", "col"), [(i, i ^ mask) for i in range(bands * cols)]
        )

    rounds = [[cols]]
    at = 1
    while at < bands * cols:
        if at == cols:
            at *= 2
            continue
        if 4 * at <= bands * cols and 2 * at != cols:
            rounds.append([at, 2 * at, 3 * at])
            at *= 4
        else:
            last = (2 * at - 1) & ~(at // 4 - 1) if len(rounds) > 3 else at
            rounds.append([last])
            at *= 2
    for masks in rounds:
        value = value + sum(from_partner(mask) for mask in masks)
    return value


def per_device(prior_basis, coupling, velocity):
    bands, cols = lax.axis_size("band"), lax.axis_size("col")
    f32, bf16 = jnp.float32, jnp.bfloat16
    basis = prior_basis.reshape(KPREV * CELL_ROWS, COLS)
    slab, to_core, to_chip, edges = pl.pallas_call(
        pack_kernel,
        out_shape=(
            OUT((ROWS, SLAB, COLS), f32),
            OUT((WIDTH, SLAB, COLS), f32),
            OUT((WIDTH, SLAB, COLS), f32),
            OUT((PACKED, 8, LANES), f32),
        ),
        in_specs=[HBM, HBM, VMEM],
        out_specs=(VMEM, VMEM, VMEM, VMEM),
        scratch_shapes=[
            pltpu.VMEM((2, BLOCK * CELL_ROWS, LANES), f32),
            pltpu.VMEM((2, COUPLINGS * ROWS, LANES), f32),
            pltpu.SemaphoreType.DMA((4,)),
        ],
        compiler_params=pltpu.CompilerParams(vmem_limit_bytes=55 * 1024 * 1024),
        name="pack",
    )(basis, coupling.reshape(COUPLINGS * ROWS, COLS), velocity)
    from_chip = row_exchange(to_chip, bands, True)
    side_even = col_exchange(edges, cols, False)
    side_odd = col_exchange(edges, cols, True)
    from_core = row_exchange(to_core, bands, False)
    prior_parts, token = pl.pallas_call(
        prior_kernel,
        out_shape=(
            OUT((ROWS, BOTH, COMPS * COLS), bf16),
            OUT((8, LANES), f32),
        ),
        in_specs=[HBM],
        out_specs=(VMEM, VMEM),
        scratch_shapes=[
            pltpu.VMEM((2, KPREV * CELL_ROWS, LANES), f32),
            pltpu.SemaphoreType.DMA((KPREV // BLOCK, 2)),
        ],
        compiler_params=pltpu.CompilerParams(vmem_limit_bytes=8 * 1024 * 1024),
        cost_estimate=pl.CostEstimate(flops=4 * 10**9, bytes_accessed=8 * 10**6, transcendentals=0),
        name="prior",
    )(basis)
    sides = pl.pallas_call(
        merge_kernel,
        out_shape=OUT((PACKED, 8, LANES), f32),
        in_specs=[VMEM, VMEM, VMEM],
        out_specs=VMEM,
        compiler_params=pltpu.CompilerParams(vmem_limit_bytes=1024 * 1024),
        name="merge",
    )(side_even, side_odd, token)
    core_sides = row_exchange(sides, bands, False)
    chip_sides = row_exchange(sides, bands, True)
    new_parts, inner = pl.pallas_call(
        power_kernel,
        out_shape=(
            OUT((ROWS, BOTH, COMPS * COLS), bf16),
            jax.ShapeDtypeStruct((KPREV + KPREV // 2, BOTH), f32),
        ),
        in_specs=[ANY, ANY, ANY, VMEM, VMEM, VMEM, VMEM],
        out_specs=(VMEM, VMEM),
        scratch_shapes=[
            pltpu.VMEM((SPAN, PLANES, WIDE), f32),
            pltpu.VMEM((SPAN, PLANES, WIDE), f32),
            pltpu.VMEM((SPAN, COEFFS, WIDE), f32),
            pltpu.SemaphoreType.DMA((6,)),
        ],
        compiler_params=pltpu.CompilerParams(vmem_limit_bytes=24 * 1024 * 1024),
        name="powers",
    )(slab, from_core, from_chip, sides, core_sides, chip_sides, prior_parts)
    inner = sum_over_devices(inner, bands, cols)
    basis_next, triangle = pl.pallas_call(
        finish_kernel,
        out_shape=(
            jax.ShapeDtypeStruct((KPREV, COMPS, ROWS, COLS), f32),
            jax.ShapeDtypeStruct((KPREV, KPREV), f32),
        ),
        in_specs=[VMEM, VMEM, VMEM],
        out_specs=(ANY, VMEM),
        scratch_shapes=[
            pltpu.VMEM((2, KPREV, COMPS, ROWS, LANES), f32),
            pltpu.SemaphoreType.DMA((COMPS, 2)),
        ],
        compiler_params=pltpu.CompilerParams(vmem_limit_bytes=24 * 1024 * 1024),
        name="finish",
    )(inner, prior_parts, new_parts)
    return (basis_next.reshape(prior_basis.shape), triangle)


def solution(mesh):
    in_specs = (
        P(None, None, None, "band", "col"),
        P(None, None, None, "band", "col"),
        P(None, "band", "col"),
    )
    out_specs = (P(None, None, None, "band", "col"), P())
    return jax.shard_map(
        per_device, mesh=mesh, in_specs=in_specs, out_specs=out_specs, check_vma=False
    )
```

time: 107 us -> 80.1 us (0.75)
  Pallas kernels: 42.5 us -> 28.6 us
  waiting for transfers between devices: 25.8 us -> 18.3 us
  starting transfers between devices: 36.1 us -> 31.2 us
  local copies, waits for them, and re-layouts: 1.34 us -> 0.01 us
    pallas_call x1, Pallas kernels: 19.7 us -> 8.29 us  [per_device(): pl.pallas_call(finish_kernel, out_shape=(jax.ShapeDtypeStruct((KPREV, COM...]
    ppermute x8 -> x11, starting transfers between devices: 26 us -> 21.1 us  [from_partner(): lax.ppermute(value, ('band', 'col'), [(i, i ^ mask) for i in range(bands...]
    ppermute x8 -> x11, waiting for transfers between devices: 20.7 us -> 16.7 us  [from_partner(): lax.ppermute(value, ('band', 'col'), [(i, i ^ mask) for i in range(bands...]
    ppermute x2, waiting for transfers between devices: 4.22 us -> 0.67 us  [col_exchange(): return lax.ppermute(value, 'col', pairs_in(cols, partner))]
    pallas_call x2 -> x4, Pallas kernels: 22.9 us -> 20.3 us  [the longest x1 13.7 us: per_device(): pl.pallas_call(power_kernel, out_shape=(OUT((ROWS, BOTH, COMPS * COLS), b...]
    unnamed x2, local copies, waits for them, and re-layouts: 1.34 us -> 0.01 us
  transfers between devices with their start and end apart: 14 -> 17, of which waited for: 11 -> 10; matrix products, arithmetic and copies ran while one was open for 0% -> 0% of each run, Pallas kernels for 0% -> 4%
where the time goes in v1:
time: 80.1 us; the launch traced here: 79.1 us
  starting transfers between devices  31.2 us (39%)
  Pallas kernels  28.6 us (36%)
  waiting for transfers between devices  18.3 us (23%)
  between operations  0.91 us (1%)
    ppermute x11, starting transfers between devices, from_partner(): lax.ppermute(value, ('band', 'col'), [(i, i ^ mask) for i in range(bands...  21.1 us
    ppermute x11, waiting for transfers between devices, from_partner(): lax.ppermute(value, ('band', 'col'), [(i, i ^ mask) for i in range(bands...  16.7 us
    pallas_call x1, Pallas kernels, per_device(): pl.pallas_call(power_kernel, out_shape=(OUT((ROWS, BOTH, COMPS * COLS), b...  13.7 us
    pallas_call x1, Pallas kernels, per_device(): pl.pallas_call(finish_kernel, out_shape=(jax.ShapeDtypeStruct((KPREV, COM...  8.29 us
    ppermute x4, starting transfers between devices, row_exchange(): return lax.ppermute(value, 'band', pairs_in(bands, partner))  6.61 us
    ppermute x2, starting transfers between devices, col_exchange(): return lax.ppermute(value, 'col', pairs_in(cols, partner))  3.49 us
    pallas_call x1, Pallas kernels, per_device(): pl.pallas_call(prior_kernel, out_shape=(OUT((ROWS, BOTH, COMPS * COLS), b...  3.33 us
    pallas_call x1, Pallas kernels, per_device(): pl.pallas_call(pack_kernel, out_shape=(OUT((ROWS, SLAB, COLS), f32), OUT(...  3.28 us
  transfers between devices with their start and end apart: 17, of which 10 were waited for; matrix products, arithmetic and copies ran while one was open for 0% of the time, Pallas kernels for 4%

profile of v1, /device:TPU:2, one launch (start us, length us, event | category | flops | bytes accessed | tf_op | source)
XLA Modules:
  0.0 79.1 jit_solution(3731069929885333075)
XLA Ops:
  0.6 0.0 copy-start
  0.6 3.3 %pack.1 = (f32[8,168,256]{2,1,0:T(8,128)S(1)}, f32[4,168,256]{2,1,0:T(8,128)S(1)}, f32[4,168,256]{2,1,0:T(8,128)S(1)}, f32[11,8,128]{2,1,0:T(8,128)S(1)}) custom-call(f32[4096,256]{1,0:T(8,128)} %bitcast.3, f32[256,256]{1,0:T(8,128)} %bitcast.5, f32[2,8,256]{2,1,0:T(8,128)} %velocity.1), custom_call_target="tpu_custom_call" | custom-call | tf_op jit(solution)/shard_map/pack/pallas_call | solution.py:403
  3.9 0.1 collective-permute-start
  4.0 0.7 collective-permute-start.1
  4.7 3.4 %collective-permute-start.3 = (f32[11,8,128]{2,1,0:T(8,128)S(1)}, f32[11,8,128]{2,1,0:T(8,128)S(1)}, u32[]{:S(2)}, u32[]{:S(2)}) collective-permute-start(f32[11,8,128]{2,1,0:T(8,128)S(1)} %get-tuple-element.15), channel_id=1, source_target_pairs={{1,2},{2,1},{5,6},{6,5},{9,10},{10,9},{13,14},{14,13},{17,18},{18,... | collective-permute-start | bytes 135176 | tf_op jit(solution)/shard_map/ppermute | solution.py:372
  8.1 0.1 collective-permute-start.2
  8.2 0.0 copy-done
  8.3 3.3 %prior.1 = (bf16[8,128,2048]{2,1,0:T(8,128)(2,1)S(1)}, f32[8,128]{1,0:T(8,128)S(1)}) custom-call(f32[4096,256]{1,0:T(8,128)S(1)} %bitcast.4), custom_call_target="tpu_custom_call" | custom-call | flops 4000000000 | bytes 8000000 | tf_op jit(solution)/shard_map/prior/pallas_call | solution.py:425
  11.6 0.0 collective-permute-done.3.side_odd
  11.6 0.7 collective-permute-done.2.side_even
  12.3 0.7 collective-permute-start.5
  13.0 5.2 %collective-permute-start.4 = (f32[11,8,128]{2,1,0:T(8,128)S(1)}, f32[11,8,128]{2,1,0:T(8,128)S(1)}, u32[]{:S(2)}, u32[]{:S(2)}) collective-permute-start(f32[11,8,128]{2,1,0:T(8,128)S(1)} %merge.1.sides), channel_id=1, source_target_pairs={{0,4},{4,0},{8,12},{12,8},{16,20},{20,16},{24,28},{28,24},{32,36},... | collective-permute-start | bytes 135176 | tf_op jit(solution)/shard_map/ppermute | solution.py:364
  18.1 0.0 collective-permute-done.5.chip_sides
  18.1 0.9 %collective-permute-done.4.core_sides = f32[11,8,128]{2,1,0:T(8,128)S(1)} collective-permute-done((f32[11,8,128]{2,1,0:T(8,128)S(1)}, f32[11,8,128]{2,1,0:T(8,128)S(1)}, u32[]{:S(2)}, u32[]{:S(2)}) %collective-permute-start.4) | collective-permute-done | bytes 45088 | tf_op jit(solution)/shard_map/ppermute | solution.py:364
  19.0 0.0 collective-permute-done.from_core
  19.0 0.0 collective-permute-done.1.from_chip
  19.0 13.7 %powers.1 = (bf16[8,128,2048]{2,1,0:T(8,128)(2,1)S(1)}, f32[96,128]{1,0:T(8,128)S(1)}) custom-call(f32[8,168,256]{2,1,0:T(8,128)S(1)} %get-tuple-element.12.slab, f32[4,168,256]{2,1,0:T(8,128)S(1)} %collective-permute-done.from_core, f32[4,168,256]{2,1,0:T(8,128)S(1)} %collective-permute-done.1.from_chip, f32[11,8,128]{2,1,0:T(8,128)S(1)} %merge.1.sides, ...), custom_call_target="tpu_custom_call" | custom-call | tf_op jit(solution)/shard_map/powers/pallas_call | solution.py:451
  32.7 0.9 %collective-permute-start.6 = (f32[96,128]{1,0:T(8,128)S(1)}, f32[96,128]{1,0:T(8,128)S(1)}, u32[]{:S(2)}, u32[]{:S(2)}) collective-permute-start(f32[96,128]{1,0:T(8,128)S(1)} %get-tuple-element.18), channel_id=1, source_target_pairs={{0,4},{1,5},{2,6},{3,7},{4,0},{5,1},{6,2},{7,3},{8,12},{9,13},{10,... | collective-permute-start | bytes 147464 | tf_op jit(solution)/shard_map/ppermute | solution.py:377
  33.6 0.9 %collective-permute-done.6 = f32[96,128]{1,0:T(8,128)S(1)} collective-permute-done((f32[96,128]{1,0:T(8,128)S(1)}, f32[96,128]{1,0:T(8,128)S(1)}, u32[]{:S(2)}, u32[]{:S(2)}) %collective-permute-start.6) | collective-permute-done | bytes 49184 | tf_op jit(solution)/shard_map/ppermute | solution.py:377
  34.4 0.5 collective-permute-start.9
  35.0 3.1 %collective-permute-start.8 = (f32[96,128]{1,0:T(8,128)S(1)}, f32[96,128]{1,0:T(8,128)S(1)}, u32[]{:S(2)}, u32[]{:S(2)}) collective-permute-start(f32[96,128]{1,0:T(8,128)S(1)} %add.33), channel_id=1, source_target_pairs={{0,2},{1,3},{2,0},{3,1},{4,6},{5,7},{6,4},{7,5},{8,10},{9,11},{10,... | collective-permute-start | bytes 147464 | tf_op jit(solution)/shard_map/ppermute | solution.py:377
  38.1 0.4 collective-permute-start.7
  38.5 0.0 collective-permute-done.9
  38.5 2.1 %collective-permute-done.8 = f32[96,128]{1,0:T(8,128)S(1)} collective-permute-done((f32[96,128]{1,0:T(8,128)S(1)}, f32[96,128]{1,0:T(8,128)S(1)}, u32[]{:S(2)}, u32[]{:S(2)}) %collective-permute-start.8) | collective-permute-done | bytes 49184 | tf_op jit(solution)/shard_map/ppermute | solution.py:377
  40.7 1.5 %collective-permute-done.7 = f32[96,128]{1,0:T(8,128)S(1)} collective-permute-done((f32[96,128]{1,0:T(8,128)S(1)}, f32[96,128]{1,0:T(8,128)S(1)}, u32[]{:S(2)}, u32[]{:S(2)}) %collective-permute-start.7) | collective-permute-done | bytes 49184 | tf_op jit(solution)/shard_map/ppermute | solution.py:377
  42.2 5.2 %collective-permute-start.12 = (f32[96,128]{1,0:T(8,128)S(1)}, f32[96,128]{1,0:T(8,128)S(1)}, u32[]{:S(2)}, u32[]{:S(2)}) collective-permute-start(f32[96,128]{1,0:T(8,128)S(1)} %add_add_fusion.2), channel_id=1, source_target_pairs={{0,24},{1,25},{2,26},{3,27},{4,28},{5,29},{6,30},{7,31},{8,16},{9,... | collective-permute-start | bytes 147464 | tf_op jit(solution)/shard_map/ppermute | solution.py:377
  47.4 0.0 collective-permute-start.11
  47.4 1.0 %collective-permute-start.10 = (f32[96,128]{1,0:T(8,128)S(1)}, f32[96,128]{1,0:T(8,128)S(1)}, u32[]{:S(2)}, u32[]{:S(2)}) collective-permute-start(f32[96,128]{1,0:T(8,128)S(1)} %add_add_fusion.2), channel_id=1, source_target_pairs={{0,8},{1,9},{2,10},{3,11},{4,12},{5,13},{6,14},{7,15},{8,0},{9,1},... | collective-permute-start | bytes 147464 | tf_op jit(solution)/shard_map/ppermute | solution.py:377
  48.4 1.1 %collective-permute-done.12 = f32[96,128]{1,0:T(8,128)S(1)} collective-permute-done((f32[96,128]{1,0:T(8,128)S(1)}, f32[96,128]{1,0:T(8,128)S(1)}, u32[]{:S(2)}, u32[]{:S(2)}) %collective-permute-start.12) | collective-permute-done | bytes 49184 | tf_op jit(solution)/shard_map/ppermute | solution.py:377
  49.5 3.5 %collective-permute-done.11 = f32[96,128]{1,0:T(8,128)S(1)} collective-permute-done((f32[96,128]{1,0:T(8,128)S(1)}, f32[96,128]{1,0:T(8,128)S(1)}, u32[]{:S(2)}, u32[]{:S(2)}) %collective-permute-start.11) | collective-permute-done | bytes 49184 | tf_op jit(solution)/shard_map/ppermute | solution.py:377
  53.0 0.0 collective-permute-done.10
  53.0 7.1 %collective-permute-start.15 = (f32[96,128]{1,0:T(8,128)S(1)}, f32[96,128]{1,0:T(8,128)S(1)}, u32[]{:S(2)}, u32[]{:S(2)}) collective-permute-start(f32[96,128]{1,0:T(8,128)S(1)} %add_add_fusion.1), channel_id=1, source_target_pairs={{0,96},{1,97},{2,98},{3,99},{4,100},{5,101},{6,102},{7,103},{8,104... | collective-permute-start | bytes 147464 | tf_op jit(solution)/shard_map/ppermute | solution.py:377
  60.2 0.0 collective-permute-start.14
  60.2 0.7 collective-permute-start.13
  60.8 1.8 %collective-permute-done.15 = f32[96,128]{1,0:T(8,128)S(1)} collective-permute-done((f32[96,128]{1,0:T(8,128)S(1)}, f32[96,128]{1,0:T(8,128)S(1)}, u32[]{:S(2)}, u32[]{:S(2)}) %collective-permute-start.15) | collective-permute-done | bytes 49184 | tf_op jit(solution)/shard_map/ppermute | solution.py:377
  62.6 2.6 %collective-permute-done.14 = f32[96,128]{1,0:T(8,128)S(1)} collective-permute-done((f32[96,128]{1,0:T(8,128)S(1)}, f32[96,128]{1,0:T(8,128)S(1)}, u32[]{:S(2)}, u32[]{:S(2)}) %collective-permute-start.14) | collective-permute-done | bytes 49184 | tf_op jit(solution)/shard_map/ppermute | solution.py:377
  65.2 0.0 collective-permute-done.13
  65.2 2.2 %collective-permute-start.16 = (f32[96,128]{1,0:T(8,128)S(1)}, f32[96,128]{1,0:T(8,128)S(1)}, u32[]{:S(2)}, u32[]{:S(2)}) collective-permute-start(f32[96,128]{1,0:T(8,128)S(1)} %add_add_fusion), channel_id=1, source_target_pairs={{0,224},{1,225},{2,226},{3,227},{4,228},{5,229},{6,230},{7,231},{8... | collective-permute-start | bytes 147464 | tf_op jit(solution)/shard_map/ppermute | solution.py:377
  67.4 3.2 %collective-permute-done.16 = f32[96,128]{1,0:T(8,128)S(1)} collective-permute-done((f32[96,128]{1,0:T(8,128)S(1)}, f32[96,128]{1,0:T(8,128)S(1)}, u32[]{:S(2)}, u32[]{:S(2)}) %collective-permute-start.16) | collective-permute-done | bytes 49184 | tf_op jit(solution)/shard_map/ppermute | solution.py:377
  70.6 8.3 %finish.1 = (f32[64,8,8,256]{3,2,1,0:T(8,128)}, f32[64,64]{1,0:T(8,128)}) custom-call(f32[96,128]{1,0:T(8,128)S(1)} %add.43.inner, bf16[8,128,2048]{2,1,0:T(8,128)(2,1)S(1)} %get-tuple-element.17.prior_parts, bf16[8,128,2048]{2,1,0:T(8,128)(2,1)S(1)} %get-tuple-element.19.new_parts), custom_call_target="tpu_custom_call" | custom-call | tf_op jit(solution)/shard_map/finish/pallas_call | solution.py:469
  (6 shorter events, 0.1 us)
Async XLA Ops:
  0.6 7.6 %copy-start = (f32[64,2,4,8,256]{4,3,2,1,0:T(8,128)S(1)}, f32[64,2,4,8,256]{4,3,2,1,0:T(8,128)}, u32[]{:S(2)}) copy-start(f32[64,2,4,8,256]{4,3,2,1,0:T(8,128)} %param.3) | copy-start | bytes 12582916
  3.9 15.1 %collective-permute-start = (f32[4,168,256]{2,1,0:T(8,128)S(1)}, f32[4,168,256]{2,1,0:T(8,128)S(1)}, u32[]{:S(2)}, u32[]{:S(2)}) collective-permute-start(f32[4,168,256]{2,1,0:T(8,128)S(1)} %get-tuple-element.13), channel_id=1, source_target_pairs={{0,4},{4,0},{8,12},{12,8},{16,20},{20,16},{24,28},{28,24},{32,36},... | collective-permute-start | bytes 2064392 | tf_op jit(solution)/shard_map/ppermute | solution.py:364
  4.0 15.0 %collective-permute-start.1 = (f32[4,168,256]{2,1,0:T(8,128)S(1)}, f32[4,168,256]{2,1,0:T(8,128)S(1)}, u32[]{:S(2)}, u32[]{:S(2)}) collective-permute-start(f32[4,168,256]{2,1,0:T(8,128)S(1)} %get-tuple-element.14), channel_id=1, source_target_pairs={{4,8},{8,4},{12,16},{16,12},{20,24},{24,20},{28,32},{32,28},{36,40... | collective-permute-start | bytes 2064392 | tf_op jit(solution)/shard_map/ppermute | solution.py:364
  4.7 6.9 %collective-permute-start.3 = (f32[11,8,128]{2,1,0:T(8,128)S(1)}, f32[11,8,128]{2,1,0:T(8,128)S(1)}, u32[]{:S(2)}, u32[]{:S(2)}) collective-permute-start(f32[11,8,128]{2,1,0:T(8,128)S(1)} %get-tuple-element.15), channel_id=1, source_target_pairs={{1,2},{2,1},{5,6},{6,5},{9,10},{10,9},{13,14},{14,13},{17,18},{18,... | collective-permute-start | bytes 135176 | tf_op jit(solution)/shard_map/ppermute | solution.py:372
  8.1 4.1 %collective-permute-start.2 = (f32[11,8,128]{2,1,0:T(8,128)S(1)}, f32[11,8,128]{2,1,0:T(8,128)S(1)}, u32[]{:S(2)}, u32[]{:S(2)}) collective-permute-start(f32[11,8,128]{2,1,0:T(8,128)S(1)} %get-tuple-element.15), channel_id=1, source_target_pairs={{0,1},{1,0},{2,3},{3,2},{4,5},{5,4},{6,7},{7,6},{8,9},{9,8},{10,11... | collective-permute-start | bytes 135176 | tf_op jit(solution)/shard_map/ppermute | solution.py:372
  12.3 5.8 %collective-permute-start.5 = (f32[11,8,128]{2,1,0:T(8,128)S(1)}, f32[11,8,128]{2,1,0:T(8,128)S(1)}, u32[]{:S(2)}, u32[]{:S(2)}) collective-permute-start(f32[11,8,128]{2,1,0:T(8,128)S(1)} %merge.1.sides), channel_id=1, source_target_pairs={{4,8},{8,4},{12,16},{16,12},{20,24},{24,20},{28,32},{32,28},{36,40... | collective-permute-start | bytes 135176 | tf_op jit(solution)/shard_map/ppermute | solution.py:364
  13.0 6.0 %collective-permute-start.4 = (f32[11,8,128]{2,1,0:T(8,128)S(1)}, f32[11,8,128]{2,1,0:T(8,128)S(1)}, u32[]{:S(2)}, u32[]{:S(2)}) collective-permute-start(f32[11,8,128]{2,1,0:T(8,128)S(1)} %merge.1.sides), channel_id=1, source_target_pairs={{0,4},{4,0},{8,12},{12,8},{16,20},{20,16},{24,28},{28,24},{32,36},... | collective-permute-start | bytes 135176 | tf_op jit(solution)/shard_map/ppermute | solution.py:364
  32.7 1.7 %collective-permute-start.6 = (f32[96,128]{1,0:T(8,128)S(1)}, f32[96,128]{1,0:T(8,128)S(1)}, u32[]{:S(2)}, u32[]{:S(2)}) collective-permute-start(f32[96,128]{1,0:T(8,128)S(1)} %get-tuple-element.18), channel_id=1, source_target_pairs={{0,4},{1,5},{2,6},{3,7},{4,0},{5,1},{6,2},{7,3},{8,12},{9,13},{10,... | collective-permute-start | bytes 147464 | tf_op jit(solution)/shard_map/ppermute | solution.py:377
  34.4 4.1 %collective-permute-start.9 = (f32[96,128]{1,0:T(8,128)S(1)}, f32[96,128]{1,0:T(8,128)S(1)}, u32[]{:S(2)}, u32[]{:S(2)}) collective-permute-start(f32[96,128]{1,0:T(8,128)S(1)} %add.33), channel_id=1, source_target_pairs={{0,3},{1,2},{2,1},{3,0},{4,7},{5,6},{6,5},{7,4},{8,11},{9,10},{10,... | collective-permute-start | bytes 147464 | tf_op jit(solution)/shard_map/ppermute | solution.py:377
  35.0 5.7 %collective-permute-start.8 = (f32[96,128]{1,0:T(8,128)S(1)}, f32[96,128]{1,0:T(8,128)S(1)}, u32[]{:S(2)}, u32[]{:S(2)}) collective-permute-start(f32[96,128]{1,0:T(8,128)S(1)} %add.33), channel_id=1, source_target_pairs={{0,2},{1,3},{2,0},{3,1},{4,6},{5,7},{6,4},{7,5},{8,10},{9,11},{10,... | collective-permute-start | bytes 147464 | tf_op jit(solution)/shard_map/ppermute | solution.py:377
  38.1 4.1 %collective-permute-start.7 = (f32[96,128]{1,0:T(8,128)S(1)}, f32[96,128]{1,0:T(8,128)S(1)}, u32[]{:S(2)}, u32[]{:S(2)}) collective-permute-start(f32[96,128]{1,0:T(8,128)S(1)} %add.33), channel_id=1, source_target_pairs={{0,1},{1,0},{2,3},{3,2},{4,5},{5,4},{6,7},{7,6},{8,9},{9,8},{10,11... | collective-permute-start | bytes 147464 | tf_op jit(solution)/shard_map/ppermute | solution.py:377
  42.2 7.3 %collective-permute-start.12 = (f32[96,128]{1,0:T(8,128)S(1)}, f32[96,128]{1,0:T(8,128)S(1)}, u32[]{:S(2)}, u32[]{:S(2)}) collective-permute-start(f32[96,128]{1,0:T(8,128)S(1)} %add_add_fusion.2), channel_id=1, source_target_pairs={{0,24},{1,25},{2,26},{3,27},{4,28},{5,29},{6,30},{7,31},{8,16},{9,... | collective-permute-start | bytes 147464 | tf_op jit(solution)/shard_map/ppermute | solution.py:377
  47.4 5.6 %collective-permute-start.11 = (f32[96,128]{1,0:T(8,128)S(1)}, f32[96,128]{1,0:T(8,128)S(1)}, u32[]{:S(2)}, u32[]{:S(2)}) collective-permute-start(f32[96,128]{1,0:T(8,128)S(1)} %add_add_fusion.2), channel_id=1, source_target_pairs={{0,16},{1,17},{2,18},{3,19},{4,20},{5,21},{6,22},{7,23},{8,24},{9,... | collective-permute-start | bytes 147464 | tf_op jit(solution)/shard_map/ppermute | solution.py:377
  47.4 5.6 %collective-permute-start.10 = (f32[96,128]{1,0:T(8,128)S(1)}, f32[96,128]{1,0:T(8,128)S(1)}, u32[]{:S(2)}, u32[]{:S(2)}) collective-permute-start(f32[96,128]{1,0:T(8,128)S(1)} %add_add_fusion.2), channel_id=1, source_target_pairs={{0,8},{1,9},{2,10},{3,11},{4,12},{5,13},{6,14},{7,15},{8,0},{9,1},... | collective-permute-start | bytes 147464 | tf_op jit(solution)/shard_map/ppermute | solution.py:377
  53.0 9.6 %collective-permute-start.15 = (f32[96,128]{1,0:T(8,128)S(1)}, f32[96,128]{1,0:T(8,128)S(1)}, u32[]{:S(2)}, u32[]{:S(2)}) collective-permute-start(f32[96,128]{1,0:T(8,128)S(1)} %add_add_fusion.1), channel_id=1, source_target_pairs={{0,96},{1,97},{2,98},{3,99},{4,100},{5,101},{6,102},{7,103},{8,104... | collective-permute-start | bytes 147464 | tf_op jit(solution)/shard_map/ppermute | solution.py:377
  60.2 5.0 %collective-permute-start.14 = (f32[96,128]{1,0:T(8,128)S(1)}, f32[96,128]{1,0:T(8,128)S(1)}, u32[]{:S(2)}, u32[]{:S(2)}) collective-permute-start(f32[96,128]{1,0:T(8,128)S(1)} %add_add_fusion.1), channel_id=1, source_target_pairs={{0,64},{1,65},{2,66},{3,67},{4,68},{5,69},{6,70},{7,71},{8,72},{9,... | collective-permute-start | bytes 147464 | tf_op jit(solution)/shard_map/ppermute | solution.py:377
  60.2 5.0 %collective-permute-start.13 = (f32[96,128]{1,0:T(8,128)S(1)}, f32[96,128]{1,0:T(8,128)S(1)}, u32[]{:S(2)}, u32[]{:S(2)}) collective-permute-start(f32[96,128]{1,0:T(8,128)S(1)} %add_add_fusion.1), channel_id=1, source_target_pairs={{0,32},{1,33},{2,34},{3,35},{4,36},{5,37},{6,38},{7,39},{8,40},{9,... | collective-permute-start | bytes 147464 | tf_op jit(solution)/shard_map/ppermute | solution.py:377
  65.2 5.4 %collective-permute-start.16 = (f32[96,128]{1,0:T(8,128)S(1)}, f32[96,128]{1,0:T(8,128)S(1)}, u32[]{:S(2)}, u32[]{:S(2)}) collective-permute-start(f32[96,128]{1,0:T(8,128)S(1)} %add_add_fusion), channel_id=1, source_target_pairs={{0,224},{1,225},{2,226},{3,227},{4,228},{5,229},{6,230},{7,231},{8... | collective-permute-start | bytes 147464 | tf_op jit(solution)/shard_map/ppermute | solution.py:377

commit v2 on v1

v2 whole, which is shorter than its diff:
```python
import math

import jax
import jax.numpy as jnp
from jax import lax
from jax.experimental import pallas as pl
from jax.experimental.pallas import tpu as pltpu
from jax.sharding import PartitionSpec as P

BLOCK = 16
STEPS = 4
KPREV = 64
COMPS = 8
ROWS = 8
COLS = 256
LANES = 128
WIDTH = 4
PLANES = COMPS * BLOCK
COUPLINGS = 32
COEFFS = 40
SLAB = PLANES + COEFFS
TILES = SLAB // 8
PACKED = (TILES + 1) // 2
SPAN = ROWS + 2 * WIDTH
STENCIL = 48
MIXING = STENCIL + 8
BOTH = 2 * KPREV
PIVOTS = 8
CELL_ROWS = COMPS * ROWS
OUT = pltpu.VMEM

ANY = pl.BlockSpec(memory_space=pl.ANY)
VMEM = pl.BlockSpec(memory_space=pltpu.VMEM)
HBM = pl.BlockSpec(memory_space=pltpu.HBM)


def core_of_chip():
    return lax.rem(lax.axis_index("band"), 2)


def pack_kernel(basis, coupling, velocity, slab, core_out, chip_out, edges, start, mixing, sems):
    size = BLOCK * 2 * CELL_ROWS
    loads = [
        pltpu.make_async_copy(basis.at[pl.ds((KPREV // BLOCK - 1) * size, size), :], start, sems.at[0]),
        pltpu.make_async_copy(coupling, mixing, sems.at[1]),
    ]
    for copy in loads:
        copy.start()
    half_rows = 0.5 * velocity[0]
    half_cols = 0.5 * velocity[1]
    stencil = (0.15 - half_rows, 0.15 + half_rows, 0.15 - half_cols, 0.15 + half_cols)
    blank = jnp.zeros((4, COLS), jnp.float32)
    for row in range(ROWS):
        slab[row, PLANES + COUPLINGS :, :] = jnp.concatenate(
            [part[row : row + 1] for part in stencil] + [blank], axis=0
        )
    for copy in loads:
        copy.wait()
    for row in range(ROWS):
        for half in range(2):
            lanes = slice(half * LANES, (half + 1) * LANES)
            for comp in range(COMPS):
                slab[row, comp * BLOCK : (comp + 1) * BLOCK, lanes] = start[
                    pl.ds((2 * comp + half) * ROWS + row, BLOCK, stride=2 * CELL_ROWS), :
                ]
            slab[row, PLANES : PLANES + COUPLINGS, lanes] = mixing[
                pl.ds(half * ROWS + row, COUPLINGS, stride=2 * ROWS), :
            ]
    core = core_of_chip()
    for row in range(WIDTH):
        core_out[row] = slab[row + (1 - core) * WIDTH]
        chip_out[row] = slab[row + core * WIDTH]
    lane = lax.broadcasted_iota(jnp.int32, (8, LANES), 1)
    for packed in range(PACKED):
        total = jnp.zeros((8, LANES), jnp.float32)
        for half in range(2):
            tile = 2 * packed + half
            if tile >= TILES:
                continue
            for row in range(ROWS):
                group = half * ROWS + row
                first = slab[row, tile * 8 : tile * 8 + 8, 0:LANES]
                last = slab[row, tile * 8 : tile * 8 + 8, COLS - LANES : COLS]
                edge = pltpu.roll(jnp.where(lane < WIDTH, first, last), (8 * group + 4) % LANES, 1)
                total = jnp.where(lane // 8 == group, edge, total)
        edges[packed] = total


def split(value):
    high = value.astype(jnp.bfloat16)
    return high, (value - high.astype(jnp.float32)).astype(jnp.bfloat16)


def prior_kernel(basis, parts, token):
    def one_row(row, carry):
        for at in range(0, KPREV, BLOCK):
            for cells in range(2 * COMPS):
                start = (at * 2 * COMPS + cells) * ROWS
                high, low = split(basis[pl.ds(start + row, BLOCK, stride=2 * CELL_ROWS), :])
                lanes = pl.ds(cells * LANES, LANES)
                parts[row, pl.ds(at, BLOCK), lanes] = high
                parts[row, pl.ds(KPREV + at, BLOCK), lanes] = low
        return carry

    lax.fori_loop(0, ROWS, one_row, 0)
    token[...] = jnp.zeros_like(token)


def merge_kernel(side_even, side_odd, edges, after, sides):
    del after
    col_is_even = lax.rem(lax.axis_index("col"), 2) == 0
    is_low = lax.broadcasted_iota(jnp.int32, edges.shape, 2) % 8 < WIDTH
    by_right = jnp.where(col_is_even, side_even[...], side_odd[...])
    by_left = jnp.where(col_is_even, side_odd[...], side_even[...])
    sides[0:PACKED] = jnp.where(is_low, by_left, edges[...])
    sides[PACKED:] = jnp.where(is_low, edges[...], by_right)


def dot_rows(a, b):
    return lax.dot_general(a, b, (((1,), (1,)), ((), ())), preferred_element_type=jnp.float32)


def join_parts(total):
    crossed = total[KPREV:, 0:KPREV] + total[0:KPREV, KPREV:]
    return total[0:KPREV, 0:KPREV] + crossed + total[KPREV:, KPREV:]


def mixing_planes(coef):
    plane = lax.broadcasted_iota(jnp.int32, (16, coef.shape[1]), 0)
    real = coef[0:16] - jnp.where(plane % 5 == 0, 0.6, 0.0)
    imag = coef[16:32]
    return jnp.concatenate([real, imag - real, imag + real, coef[COUPLINGS:]], axis=0)


def advance(center, around, coeff, store):
    both = [center[field] + center[4 + field] for field in range(4)]
    for field in range(4):
        shared = around_real = around_imag = None
        for source in range(4):
            plane = field * 4 + source
            terms = (
                coeff(plane) * both[source],
                coeff(16 + plane) * center[source],
                coeff(32 + plane) * center[4 + source],
            )
            if source == 0:
                shared, around_imag, around_real = terms
            else:
                shared = shared + terms[0]
                around_imag = around_imag + terms[1]
                around_real = around_real + terms[2]
        store(field, around(field) + (shared - around_real))
        store(4 + field, around(4 + field) + (shared + around_imag))


def spread(value):
    return jnp.concatenate([value, value], axis=0)


def operator_row(cur, nxt, outside, mix, row):
    lane = lax.broadcasted_iota(jnp.int32, (BLOCK, LANES), 1)
    is_first, is_last = lane == 0, lane == LANES - 1

    def planes(comp):
        return pl.ds(comp * BLOCK, BLOCK)

    beyond = [pltpu.roll(outside[planes(comp), :], LANES - 4 - 8 * row, 1) for comp in range(COMPS)]
    for tile in range(2):
        lanes, others = pl.ds(tile * LANES, LANES), pl.ds((1 - tile) * LANES, LANES)
        center = [cur[row, planes(comp), lanes] for comp in range(COMPS)]

        def coeff(plane, tile=tile):
            return spread(mix[tile, row, pl.ds(plane, 8, stride=0), :])

        def around(comp, tile=tile, lanes=lanes, others=others, center=center, coeff=coeff):
            other = cur[row, planes(comp), others]
            after, before = (other, beyond[comp]) if tile == 0 else (beyond[comp], other)
            right = pltpu.roll(jnp.where(is_first, after, center[comp]), LANES - 1, 1)
            left = pltpu.roll(jnp.where(is_last, before, center[comp]), 1, 1)
            return (
                coeff(STENCIL) * cur[row + 1, planes(comp), lanes]
                + coeff(STENCIL + 1) * cur[row - 1, planes(comp), lanes]
                + coeff(STENCIL + 2) * right
                + coeff(STENCIL + 3) * left
            )

        def store(comp, value, lanes=lanes):
            nxt[row, planes(comp), lanes] = value

        advance(center, around, coeff, store)


def operator_strip(strip, strip_next, strip_mix, side):
    def planes(comp):
        return pl.ds(comp * BLOCK, BLOCK)

    def coeff(plane):
        return spread(strip_mix[side, pl.ds(plane, 8, stride=0), :])

    center = [strip[side, planes(comp), :] for comp in range(COMPS)]

    def around(comp):
        here = center[comp]
        return (
            coeff(STENCIL) * pltpu.roll(here, LANES - 8, 1)
            + coeff(STENCIL + 1) * pltpu.roll(here, 8, 1)
            + coeff(STENCIL + 2) * pltpu.roll(here, LANES - 1, 1)
            + coeff(STENCIL + 3) * pltpu.roll(here, 1, 1)
        )

    def store(comp, value):
        strip_next[side, planes(comp), :] = value

    advance(center, around, coeff, store)


def join_strips(strip, outside):
    lane = lax.broadcasted_iota(jnp.int32, outside.shape, 1)
    outside[...] = jnp.where(lane % 8 < WIDTH, strip[0], strip[1])


def power_kernel(
    slab, from_core, from_chip, sides, core_sides, chip_sides, prior_parts,
    parts, inner_out,
    ping, pong, coef, mix, strip_ping, strip_pong, strip_mix, outside, halo_sems,
):
    core = core_of_chip()
    is_first = core == 0
    core_at = pl.multiple_of((1 - core) * (SPAN - WIDTH), WIDTH)
    chip_at = pl.multiple_of(core * (SPAN - WIDTH), WIDTH)
    halos = []
    for index, (source, where, count) in enumerate(
        ((slab, WIDTH, ROWS), (from_core, core_at, WIDTH), (from_chip, chip_at, WIDTH))
    ):
        halos.append(
            pltpu.make_async_copy(
                source.at[:, pl.ds(0, PLANES), :],
                ping.at[pl.ds(where, count)],
                halo_sems.at[2 * index],
            )
        )
        halos.append(
            pltpu.make_async_copy(
                source.at[:, pl.ds(PLANES, COEFFS), :],
                coef.at[pl.ds(where, count)],
                halo_sems.at[2 * index + 1],
            )
        )
    for copy in halos:
        copy.start()
    lane = lax.broadcasted_iota(jnp.int32, (8, LANES), 1)
    for side in range(2):
        strip_coef = []
        for tile in range(TILES):
            packed, at = side * PACKED + tile // 2, tile % 2 * (LANES // 2)
            by_core, by_chip = core_sides[packed], chip_sides[packed]
            above = pltpu.roll(jnp.where(is_first, by_core, by_chip), (3 * LANES // 4 - at) % LANES, 1)
            below = pltpu.roll(
                jnp.where(is_first, by_chip, by_core), (LANES - at - LANES // 4) % LANES, 1
            )
            own = pltpu.roll(sides[packed], (LANES + LANES // 4 - at) % LANES, 1)
            strip = jnp.where(lane < LANES // 4, below, jnp.where(lane < 3 * LANES // 4, own, above))
            if tile < PLANES // 8:
                strip_ping[side, tile * 8 : tile * 8 + 8] = strip
            else:
                strip_coef.append(strip)
        strip_mix[side, 0:MIXING] = mixing_planes(jnp.concatenate(strip_coef, axis=0))
    for copy in halos:
        copy.wait()

    def one_mix(row, carry):
        for tile in range(2):
            mix[tile, row, 0:MIXING] = mixing_planes(coef[row, :, pl.ds(tile * LANES, LANES)])
        return carry

    lax.fori_loop(0, SPAN, one_mix, 0, unroll=4)
    buffers = ((ping, strip_ping), (pong, strip_pong))
    for step in range(1, STEPS + 1):
        (cur, strip), (nxt, strip_next) = buffers[(step - 1) % 2], buffers[step % 2]

        join_strips(strip, outside)

        def one_row(row, carry, cur=cur, nxt=nxt):
            operator_row(cur, nxt, outside, mix, row)
            return carry

        lax.fori_loop(step, SPAN - step, one_row, 0, unroll=True)
        if step < STEPS:
            for side in range(2):
                operator_strip(strip, strip_next, strip_mix, side)

        def one_split(row, carry, nxt=nxt, step=step):
            at = (step - 1) * BLOCK
            for comp in range(COMPS):
                high, low = split(nxt[row + WIDTH, pl.ds(comp * BLOCK, BLOCK), :])
                parts[row, pl.ds(at, BLOCK), pl.ds(comp * COLS, COLS)] = high
                parts[row, pl.ds(KPREV + at, BLOCK), pl.ds(comp * COLS, COLS)] = low
            return carry

        lax.fori_loop(0, ROWS, one_split, 0, unroll=True)
    total = 0.0
    for row in range(ROWS):
        block = jnp.concatenate([prior_parts[row], parts[row]], axis=0)
        total = total + dot_rows(block, block)
    inner_out[0:KPREV] = jnp.concatenate(
        [join_parts(total[:BOTH, :BOTH]), join_parts(total[:BOTH, BOTH:])], axis=1
    )
    new = join_parts(total[BOTH:, BOTH:])
    inner_out[KPREV:] = jnp.concatenate([new[: KPREV // 2], new[KPREV // 2 :]], axis=1)


def finish_kernel(inner, prior_parts, new_parts, basis_out, triangle_out, result, out_sems):
    def dot(a, b, dims):
        return lax.dot_general(
            a, b, (dims, ((), ())), precision=lax.Precision.HIGHEST, preferred_element_type=jnp.float32
        )

    prior = inner[0:KPREV, 0:KPREV]
    coeffs = inner[0:KPREV, KPREV:]
    new = jnp.concatenate([inner[KPREV:, 0:KPREV], inner[KPREV:, KPREV:]], axis=0)
    mixed = dot(prior, coeffs, ((1,), (0,))) - 2.0 * coeffs
    gram = new + dot(coeffs, mixed, ((0,), (0,)))
    col_id = lax.broadcasted_iota(jnp.int32, (KPREV, 2 * KPREV), 1)
    unit = jnp.where(
        lax.broadcasted_iota(jnp.int32, (KPREV, KPREV), 0)
        == lax.broadcasted_iota(jnp.int32, (KPREV, KPREV), 1),
        1.0,
        0.0,
    )
    work = jnp.concatenate([gram, unit], axis=1)
    done = []
    for pivot in range(0, KPREV, PIVOTS):
        top = pivot // 8 * 8
        if pivot % 8 == 0 and pivot:
            done.append(work[:8])
            work = work[8:]
        at = pivot - top
        row_id = lax.broadcasted_iota(jnp.int32, work.shape, 0)
        columns = [
            jnp.broadcast_to(work[:, pivot + i : pivot + i + 1], work.shape) for i in range(PIVOTS)
        ]
        rows = [work[at + i : at + i + 1] for i in range(PIVOTS)]
        for i in range(PIVOTS):
            column = columns[i]
            factor = jnp.where(row_id > at + i, column * (1.0 / column[at + i : at + i + 1]), 0.0)
            work = work - factor * rows[i]
            for j in range(i + 1, PIVOTS):
                rows[j] = rows[j] - factor[at + j : at + j + 1] * rows[i]
                columns[j] = columns[j] - factor * columns[j][at + i : at + i + 1]
    work = jnp.concatenate(done + [work], axis=0)
    row_id = lax.broadcasted_iota(jnp.int32, (KPREV, 2 * KPREV), 0)
    diagonal = jnp.sum(jnp.where(row_id == col_id, work, 0.0), axis=1, keepdims=True)
    work = work / jnp.sqrt(diagonal)
    upper = work[:, :KPREV]
    triangle_out[...] = jnp.where(col_id[:, :KPREV] >= row_id[:, :KPREV], upper, 0.0)
    unknowns = 2 * 4 * 512 * 1024
    inverse = work[:, KPREV:] * math.sqrt(unknowns)
    weights = jnp.concatenate(
        [two_parts(-dot(inverse, coeffs, ((1,), (1,)))), two_parts(inverse)], axis=1
    )
    rows = result.reshape(KPREV * 2 * CELL_ROWS, LANES)
    stores = []
    for comp in range(COMPS):
        cells = slice(comp * COLS, (comp + 1) * COLS)
        for row in range(ROWS):
            vectors = jnp.concatenate([prior_parts[row, :, cells], new_parts[row, :, cells]], axis=0)
            both = jnp.dot(weights, vectors, preferred_element_type=jnp.float32)
            both = both[:KPREV] + both[KPREV:]
            for half in range(2):
                where = pl.ds((comp * 2 + half) * ROWS + row, KPREV, stride=2 * CELL_ROWS)
                rows[where, :] = both[:, half * LANES : (half + 1) * LANES]
        copy = pltpu.make_async_copy(result.at[:, comp], basis_out.at[:, comp], out_sems.at[comp])
        copy.start()
        stores.append(copy)
    for copy in stores:
        copy.wait()


def two_parts(weights):
    high, low = split(weights)
    return jnp.concatenate(
        [
            jnp.concatenate([high, high], axis=1),
            jnp.concatenate([low, jnp.zeros_like(low)], axis=1),
        ],
        axis=0,
    )


def pairs_in(size, partner):
    return [(i, partner(i)) for i in range(size) if partner(i) is not None]


def row_exchange(value, bands, across):
    def partner(i):
        j = i + (1 if (i % 2 == 0) == (not across) else -1)
        return j if 0 <= j < bands else None

    return lax.ppermute(value, "band", pairs_in(bands, partner))


def col_exchange(value, cols, odd):
    def partner(i):
        j = i + (1 if (i % 2 == 0) == (not odd) else -1)
        return j if 0 <= j < cols else None

    return lax.ppermute(value, "col", pairs_in(cols, partner))


def sum_over_devices(value, bands, cols):
    def from_partner(mask):
        return lax.ppermute(
            value, ("band", "col"), [(i, i ^ mask) for i in range(bands * cols)]
        )

    rounds = [[cols]]
    at = 1
    while at < bands * cols:
        if at == cols:
            at *= 2
            continue
        if 4 * at <= bands * cols and 2 * at != cols:
            rounds.append([at, 2 * at, 3 * at])
            at *= 4
        else:
            last = (2 * at - 1) & ~(at // 4 - 1) if len(rounds) > 3 else at
            rounds.append([last])
            at *= 2
    for masks in rounds:
        value = value + sum(from_partner(mask) for mask in masks)
    return value


def per_device(prior_basis, coupling, velocity):
    bands, cols = lax.axis_size("band"), lax.axis_size("col")
    f32, bf16 = jnp.float32, jnp.bfloat16
    basis = prior_basis.reshape(KPREV, COMPS, ROWS, 2, LANES).swapaxes(2, 3)
    slab, to_core, to_chip, edges = pl.pallas_call(
        pack_kernel,
        out_shape=(
            OUT((ROWS, SLAB, COLS), f32),
            OUT((WIDTH, SLAB, COLS), f32),
            OUT((WIDTH, SLAB, COLS), f32),
            OUT((PACKED, 8, LANES), f32),
        ),
        in_specs=[HBM, HBM, VMEM],
        out_specs=(VMEM, VMEM, VMEM, VMEM),
        scratch_shapes=[
            pltpu.VMEM((BLOCK * CELL_ROWS * 2, LANES), f32),
            pltpu.VMEM((COUPLINGS * ROWS * 2, LANES), f32),
            pltpu.SemaphoreType.DMA((2,)),
        ],
        compiler_params=pltpu.CompilerParams(vmem_limit_bytes=55 * 1024 * 1024),
        name="pack",
    )(
        basis.reshape(KPREV * CELL_ROWS * 2, LANES),
        coupling.reshape(COUPLINGS, ROWS, 2, LANES).swapaxes(1, 2).reshape(COUPLINGS * ROWS * 2, LANES),
        velocity,
    )
    from_chip = row_exchange(to_chip, bands, True)
    side_even = col_exchange(edges, cols, False)
    side_odd = col_exchange(edges, cols, True)
    from_core = row_exchange(to_core, bands, False)
    prior_parts, token = pl.pallas_call(
        prior_kernel,
        out_shape=(
            OUT((ROWS, BOTH, COMPS * COLS), bf16),
            OUT((8, LANES), f32),
        ),
        in_specs=[VMEM],
        out_specs=(VMEM, VMEM),
        compiler_params=pltpu.CompilerParams(vmem_limit_bytes=8 * 1024 * 1024),
        cost_estimate=pl.CostEstimate(flops=4 * 10**9, bytes_accessed=8 * 10**6, transcendentals=0),
        name="prior",
    )(basis.reshape(KPREV * CELL_ROWS * 2, LANES))
    sides = pl.pallas_call(
        merge_kernel,
        out_shape=OUT((2 * PACKED, 8, LANES), f32),
        in_specs=[VMEM, VMEM, VMEM, VMEM],
        out_specs=VMEM,
        compiler_params=pltpu.CompilerParams(vmem_limit_bytes=1024 * 1024),
        name="merge",
    )(side_even, side_odd, edges, token)
    core_sides = row_exchange(sides, bands, False)
    chip_sides = row_exchange(sides, bands, True)
    new_parts, inner = pl.pallas_call(
        power_kernel,
        out_shape=(
            OUT((ROWS, BOTH, COMPS * COLS), bf16),
            jax.ShapeDtypeStruct((KPREV + KPREV // 2, BOTH), f32),
        ),
        in_specs=[ANY, ANY, ANY, VMEM, VMEM, VMEM, VMEM],
        out_specs=(VMEM, VMEM),
        scratch_shapes=[
            pltpu.VMEM((SPAN, PLANES, COLS), f32),
            pltpu.VMEM((SPAN, PLANES, COLS), f32),
            pltpu.VMEM((SPAN, COEFFS, COLS), f32),
            pltpu.VMEM((2, SPAN, MIXING + 8, LANES), f32),
            pltpu.VMEM((2, PLANES, LANES), f32),
            pltpu.VMEM((2, PLANES, LANES), f32),
            pltpu.VMEM((2, MIXING + 8, LANES), f32),
            pltpu.VMEM((PLANES, LANES), f32),
            pltpu.SemaphoreType.DMA((6,)),
        ],
        compiler_params=pltpu.CompilerParams(vmem_limit_bytes=24 * 1024 * 1024),
        name="powers",
    )(slab, from_core, from_chip, sides, core_sides, chip_sides, prior_parts)
    inner = sum_over_devices(inner, bands, cols)
    basis_next, triangle = pl.pallas_call(
        finish_kernel,
        out_shape=(
            jax.ShapeDtypeStruct((KPREV, COMPS, 2, ROWS, LANES), f32),
            jax.ShapeDtypeStruct((KPREV, KPREV), f32),
        ),
        in_specs=[VMEM, VMEM, VMEM],
        out_specs=(ANY, VMEM),
        scratch_shapes=[
            pltpu.VMEM((KPREV, COMPS, 2, ROWS, LANES), f32),
            pltpu.SemaphoreType.DMA((COMPS,)),
        ],
        compiler_params=pltpu.CompilerParams(vmem_limit_bytes=24 * 1024 * 1024),
        name="finish",
    )(inner, prior_parts, new_parts)
    basis_next = basis_next.swapaxes(2, 3).reshape(prior_basis.shape)
    return (basis_next, triangle)


def solution(mesh):
    in_specs = (
        P(None, None, None, "band", "col"),
        P(None, None, None, "band", "col"),
        P(None, "band", "col"),
    )
    out_specs = (P(None, None, None, "band", "col"), P())
    return jax.shard_map(
        per_device, mesh=mesh, in_specs=in_specs, out_specs=out_specs, check_vma=False
    )
```

time: 80.1 us -> 75.4 us (0.941)
  Pallas kernels: 28.6 us -> 23.2 us
    pallas_call x1, Pallas kernels: 13.7 us -> 9.3 us  [per_device(): pl.pallas_call(power_kernel, out_shape=(OUT((ROWS, BOTH, COMPS * COLS), b...]
where the time goes in v2:
time: 75.4 us; the launch traced here: 74.3 us
  starting transfers between devices  31.8 us (42%)
  Pallas kernels  23.2 us (31%)
  waiting for transfers between devices  18.4 us (24%)
  between operations  0.91 us (1%)
    ppermute x11, starting transfers between devices, from_partner(): lax.ppermute(value, ('band', 'col'), [(i, i ^ mask) for i in range(bands...  21.7 us
    ppermute x11, waiting for transfers between devices, from_partner(): lax.ppermute(value, ('band', 'col'), [(i, i ^ mask) for i in range(bands...  16.2 us
    pallas_call x1, Pallas kernels, per_device(): pl.pallas_call(power_kernel, out_shape=(OUT((ROWS, BOTH, COMPS * COLS), b...  9.3 us
    pallas_call x1, Pallas kernels, per_device(): pl.pallas_call(finish_kernel, out_shape=(jax.ShapeDtypeStruct((KPREV, COM...  7.86 us
    ppermute x4, starting transfers between devices, row_exchange(): return lax.ppermute(value, 'band', pairs_in(bands, partner))  6.61 us
    ppermute x2, starting transfers between devices, col_exchange(): return lax.ppermute(value, 'col', pairs_in(cols, partner))  3.49 us
    pallas_call x1, Pallas kernels, per_device(): pl.pallas_call(pack_kernel, out_shape=(OUT((ROWS, SLAB, COLS), f32), OUT(...  3.29 us
    pallas_call x1, Pallas kernels, per_device(): pl.pallas_call(prior_kernel, out_shape=(OUT((ROWS, BOTH, COMPS * COLS), b...  2.75 us
  transfers between devices with their start and end apart: 17, of which 10 were waited for; matrix products, arithmetic and copies ran while one was open for 0% of the time, Pallas kernels for 4%

profile of v2, /device:TPU:2, one launch (start us, length us, event | category | flops | bytes accessed | tf_op | source)
XLA Modules:
  0.0 74.3 jit_solution(2164828201026284504)
XLA Ops:
  0.6 0.0 copy-start
  0.6 3.3 %pack.1 = (f32[8,168,256]{2,1,0:T(8,128)S(1)}, f32[4,168,256]{2,1,0:T(8,128)S(1)}, f32[4,168,256]{2,1,0:T(8,128)S(1)}, f32[11,8,128]{2,1,0:T(8,128)S(1)}) custom-call(f32[8192,128]{1,0:T(8,128)} %bitcast.13, f32[512,128]{1,0:T(8,128)} %bitcast.15, f32[2,8,256]{2,1,0:T(8,128)} %velocity.1), custom_call_target="tpu_custom_call" | custom-call | tf_op jit(solution)/shard_map/pack/pallas_call | solution.py:438
  3.9 0.1 collective-permute-start
  4.0 0.7 collective-permute-start.1
  4.8 3.4 %collective-permute-start.3 = (f32[11,8,128]{2,1,0:T(8,128)S(1)}, f32[11,8,128]{2,1,0:T(8,128)S(1)}, u32[]{:S(2)}, u32[]{:S(2)}) collective-permute-start(f32[11,8,128]{2,1,0:T(8,128)S(1)} %get-tuple-element.15.edges), channel_id=1, source_target_pairs={{1,2},{2,1},{5,6},{6,5},{9,10},{10,9},{13,14},{14,13},{17,18},{18,... | collective-permute-start | bytes 135176 | tf_op jit(solution)/shard_map/ppermute | solution.py:407
  8.2 0.1 collective-permute-start.2
  8.3 0.0 copy-done
  8.3 2.8 %prior.1 = (bf16[8,128,2048]{2,1,0:T(8,128)(2,1)S(1)}, f32[8,128]{1,0:T(8,128)S(1)}) custom-call(f32[8192,128]{1,0:T(8,128)S(1)} %bitcast.14), custom_call_target="tpu_custom_call" | custom-call | flops 4000000000 | bytes 8000000 | tf_op jit(solution)/shard_map/prior/pallas_call | solution.py:464
  11.0 0.0 collective-permute-done.3.side_odd
  11.0 1.3 %collective-permute-done.2.side_even = f32[11,8,128]{2,1,0:T(8,128)S(1)} collective-permute-done((f32[11,8,128]{2,1,0:T(8,128)S(1)}, f32[11,8,128]{2,1,0:T(8,128)S(1)}, u32[]{:S(2)}, u32[]{:S(2)}) %collective-permute-start.2) | collective-permute-done | bytes 45088 | tf_op jit(solution)/shard_map/ppermute | solution.py:407
  12.3 0.7 collective-permute-start.5
  13.0 5.1 %collective-permute-start.4 = (f32[22,8,128]{2,1,0:T(8,128)S(1)}, f32[22,8,128]{2,1,0:T(8,128)S(1)}, u32[]{:S(2)}, u32[]{:S(2)}) collective-permute-start(f32[22,8,128]{2,1,0:T(8,128)S(1)} %merge.1.sides), channel_id=1, source_target_pairs={{0,4},{4,0},{8,12},{12,8},{16,20},{20,16},{24,28},{28,24},{32,36},... | collective-permute-start | bytes 270344 | tf_op jit(solution)/shard_map/ppermute | solution.py:399
  18.1 0.0 collective-permute-done.5.chip_sides
  18.1 0.9 %collective-permute-done.4.core_sides = f32[22,8,128]{2,1,0:T(8,128)S(1)} collective-permute-done((f32[22,8,128]{2,1,0:T(8,128)S(1)}, f32[22,8,128]{2,1,0:T(8,128)S(1)}, u32[]{:S(2)}, u32[]{:S(2)}) %collective-permute-start.4) | collective-permute-done | bytes 90144 | tf_op jit(solution)/shard_map/ppermute | solution.py:399
  19.1 0.0 collective-permute-done.from_core
  19.1 0.0 collective-permute-done.1.from_chip
  19.1 9.3 %powers.1 = (bf16[8,128,2048]{2,1,0:T(8,128)(2,1)S(1)}, f32[96,128]{1,0:T(8,128)S(1)}) custom-call(f32[8,168,256]{2,1,0:T(8,128)S(1)} %get-tuple-element.12.slab, f32[4,168,256]{2,1,0:T(8,128)S(1)} %collective-permute-done.from_core, f32[4,168,256]{2,1,0:T(8,128)S(1)} %collective-permute-done.1.from_chip, f32[22,8,128]{2,1,0:T(8,128)S(1)} %merge.1.sides, ...), custom_call_target="tpu_custom_call" | custom-call | tf_op jit(solution)/shard_map/powers/pallas_call | solution.py:486
  28.4 1.5 %collective-permute-start.6 = (f32[96,128]{1,0:T(8,128)S(1)}, f32[96,128]{1,0:T(8,128)S(1)}, u32[]{:S(2)}, u32[]{:S(2)}) collective-permute-start(f32[96,128]{1,0:T(8,128)S(1)} %get-tuple-element.18), channel_id=1, source_target_pairs={{0,4},{1,5},{2,6},{3,7},{4,0},{5,1},{6,2},{7,3},{8,12},{9,13},{10,... | collective-permute-start | bytes 147464 | tf_op jit(solution)/shard_map/ppermute | solution.py:412
  29.9 0.9 %collective-permute-done.6 = f32[96,128]{1,0:T(8,128)S(1)} collective-permute-done((f32[96,128]{1,0:T(8,128)S(1)}, f32[96,128]{1,0:T(8,128)S(1)}, u32[]{:S(2)}, u32[]{:S(2)}) %collective-permute-start.6) | collective-permute-done | bytes 49184 | tf_op jit(solution)/shard_map/ppermute | solution.py:412
  30.7 0.5 collective-permute-start.9
  31.3 2.6 %collective-permute-start.8 = (f32[96,128]{1,0:T(8,128)S(1)}, f32[96,128]{1,0:T(8,128)S(1)}, u32[]{:S(2)}, u32[]{:S(2)}) collective-permute-start(f32[96,128]{1,0:T(8,128)S(1)} %add.33), channel_id=1, source_target_pairs={{0,2},{1,3},{2,0},{3,1},{4,6},{5,7},{6,4},{7,5},{8,10},{9,11},{10,... | collective-permute-start | bytes 147464 | tf_op jit(solution)/shard_map/ppermute | solution.py:412
  33.8 1.0 %collective-permute-start.7 = (f32[96,128]{1,0:T(8,128)S(1)}, f32[96,128]{1,0:T(8,128)S(1)}, u32[]{:S(2)}, u32[]{:S(2)}) collective-permute-start(f32[96,128]{1,0:T(8,128)S(1)} %add.33), channel_id=1, source_target_pairs={{0,1},{1,0},{2,3},{3,2},{4,5},{5,4},{6,7},{7,6},{8,9},{9,8},{10,11... | collective-permute-start | bytes 147464 | tf_op jit(solution)/shard_map/ppermute | solution.py:412
  34.8 0.0 collective-permute-done.9
  34.8 2.5 %collective-permute-done.8 = f32[96,128]{1,0:T(8,128)S(1)} collective-permute-done((f32[96,128]{1,0:T(8,128)S(1)}, f32[96,128]{1,0:T(8,128)S(1)}, u32[]{:S(2)}, u32[]{:S(2)}) %collective-permute-start.8) | collective-permute-done | bytes 49184 | tf_op jit(solution)/shard_map/ppermute | solution.py:412
  37.3 0.6 collective-permute-done.7
  37.9 5.2 %collective-permute-start.12 = (f32[96,128]{1,0:T(8,128)S(1)}, f32[96,128]{1,0:T(8,128)S(1)}, u32[]{:S(2)}, u32[]{:S(2)}) collective-permute-start(f32[96,128]{1,0:T(8,128)S(1)} %add_add_fusion.2), channel_id=1, source_target_pairs={{0,24},{1,25},{2,26},{3,27},{4,28},{5,29},{6,30},{7,31},{8,16},{9,... | collective-permute-start | bytes 147464 | tf_op jit(solution)/shard_map/ppermute | solution.py:412
  43.1 0.0 collective-permute-start.11
  43.1 1.0 %collective-permute-start.10 = (f32[96,128]{1,0:T(8,128)S(1)}, f32[96,128]{1,0:T(8,128)S(1)}, u32[]{:S(2)}, u32[]{:S(2)}) collective-permute-start(f32[96,128]{1,0:T(8,128)S(1)} %add_add_fusion.2), channel_id=1, source_target_pairs={{0,8},{1,9},{2,10},{3,11},{4,12},{5,13},{6,14},{7,15},{8,0},{9,1},... | collective-permute-start | bytes 147464 | tf_op jit(solution)/shard_map/ppermute | solution.py:412
  44.1 1.1 %collective-permute-done.12 = f32[96,128]{1,0:T(8,128)S(1)} collective-permute-done((f32[96,128]{1,0:T(8,128)S(1)}, f32[96,128]{1,0:T(8,128)S(1)}, u32[]{:S(2)}, u32[]{:S(2)}) %collective-permute-start.12) | collective-permute-done | bytes 49184 | tf_op jit(solution)/shard_map/ppermute | solution.py:412
  45.2 3.5 %collective-permute-done.11 = f32[96,128]{1,0:T(8,128)S(1)} collective-permute-done((f32[96,128]{1,0:T(8,128)S(1)}, f32[96,128]{1,0:T(8,128)S(1)}, u32[]{:S(2)}, u32[]{:S(2)}) %collective-permute-start.11) | collective-permute-done | bytes 49184 | tf_op jit(solution)/shard_map/ppermute | solution.py:412
  48.7 0.0 collective-permute-done.10
  48.8 7.1 %collective-permute-start.15 = (f32[96,128]{1,0:T(8,128)S(1)}, f32[96,128]{1,0:T(8,128)S(1)}, u32[]{:S(2)}, u32[]{:S(2)}) collective-permute-start(f32[96,128]{1,0:T(8,128)S(1)} %add_add_fusion.1), channel_id=1, source_target_pairs={{0,96},{1,97},{2,98},{3,99},{4,100},{5,101},{6,102},{7,103},{8,104... | collective-permute-start | bytes 147464 | tf_op jit(solution)/shard_map/ppermute | solution.py:412
  55.9 0.0 collective-permute-start.14
  55.9 0.7 collective-permute-start.13
  56.5 1.5 %collective-permute-done.15 = f32[96,128]{1,0:T(8,128)S(1)} collective-permute-done((f32[96,128]{1,0:T(8,128)S(1)}, f32[96,128]{1,0:T(8,128)S(1)}, u32[]{:S(2)}, u32[]{:S(2)}) %collective-permute-start.15) | collective-permute-done | bytes 49184 | tf_op jit(solution)/shard_map/ppermute | solution.py:412
  58.1 2.8 %collective-permute-done.14 = f32[96,128]{1,0:T(8,128)S(1)} collective-permute-done((f32[96,128]{1,0:T(8,128)S(1)}, f32[96,128]{1,0:T(8,128)S(1)}, u32[]{:S(2)}, u32[]{:S(2)}) %collective-permute-start.14) | collective-permute-done | bytes 49184 | tf_op jit(solution)/shard_map/ppermute | solution.py:412
  60.9 0.0 collective-permute-done.13
  60.9 2.1 %collective-permute-start.16 = (f32[96,128]{1,0:T(8,128)S(1)}, f32[96,128]{1,0:T(8,128)S(1)}, u32[]{:S(2)}, u32[]{:S(2)}) collective-permute-start(f32[96,128]{1,0:T(8,128)S(1)} %add_add_fusion), channel_id=1, source_target_pairs={{0,224},{1,225},{2,226},{3,227},{4,228},{5,229},{6,230},{7,231},{8... | collective-permute-start | bytes 147464 | tf_op jit(solution)/shard_map/ppermute | solution.py:412
  63.0 3.3 %collective-permute-done.16 = f32[96,128]{1,0:T(8,128)S(1)} collective-permute-done((f32[96,128]{1,0:T(8,128)S(1)}, f32[96,128]{1,0:T(8,128)S(1)}, u32[]{:S(2)}, u32[]{:S(2)}) %collective-permute-start.16) | collective-permute-done | bytes 49184 | tf_op jit(solution)/shard_map/ppermute | solution.py:412
  66.3 7.9 %finish.1 = (f32[64,8,2,8,128]{4,3,2,1,0:T(8,128)}, f32[64,64]{1,0:T(8,128)}) custom-call(f32[96,128]{1,0:T(8,128)S(1)} %add.43.inner, bf16[8,128,2048]{2,1,0:T(8,128)(2,1)S(1)} %get-tuple-element.17.prior_parts, bf16[8,128,2048]{2,1,0:T(8,128)(2,1)S(1)} %get-tuple-element.19.new_parts), custom_call_target="tpu_custom_call" | custom-call | tf_op jit(solution)/shard_map/finish/pallas_call | solution.py:509
  (6 shorter events, 0.1 us)
Async XLA Ops:
  0.6 7.6 %copy-start = (f32[64,2,4,8,256]{4,3,2,1,0:T(8,128)S(1)}, f32[64,2,4,8,256]{4,3,2,1,0:T(8,128)}, u32[]{:S(2)}) copy-start(f32[64,2,4,8,256]{4,3,2,1,0:T(8,128)} %param.3) | copy-start | bytes 12582916
  3.9 15.1 %collective-permute-start = (f32[4,168,256]{2,1,0:T(8,128)S(1)}, f32[4,168,256]{2,1,0:T(8,128)S(1)}, u32[]{:S(2)}, u32[]{:S(2)}) collective-permute-start(f32[4,168,256]{2,1,0:T(8,128)S(1)} %get-tuple-element.13), channel_id=1, source_target_pairs={{0,4},{4,0},{8,12},{12,8},{16,20},{20,16},{24,28},{28,24},{32,36},... | collective-permute-start | bytes 2064392 | tf_op jit(solution)/shard_map/ppermute | solution.py:399
  4.0 15.0 %collective-permute-start.1 = (f32[4,168,256]{2,1,0:T(8,128)S(1)}, f32[4,168,256]{2,1,0:T(8,128)S(1)}, u32[]{:S(2)}, u32[]{:S(2)}) collective-permute-start(f32[4,168,256]{2,1,0:T(8,128)S(1)} %get-tuple-element.14), channel_id=1, source_target_pairs={{4,8},{8,4},{12,16},{16,12},{20,24},{24,20},{28,32},{32,28},{36,40... | collective-permute-start | bytes 2064392 | tf_op jit(solution)/shard_map/ppermute | solution.py:399
  4.8 6.3 %collective-permute-start.3 = (f32[11,8,128]{2,1,0:T(8,128)S(1)}, f32[11,8,128]{2,1,0:T(8,128)S(1)}, u32[]{:S(2)}, u32[]{:S(2)}) collective-permute-start(f32[11,8,128]{2,1,0:T(8,128)S(1)} %get-tuple-element.15.edges), channel_id=1, source_target_pairs={{1,2},{2,1},{5,6},{6,5},{9,10},{10,9},{13,14},{14,13},{17,18},{18,... | collective-permute-start | bytes 135176 | tf_op jit(solution)/shard_map/ppermute | solution.py:407
  8.2 4.1 %collective-permute-start.2 = (f32[11,8,128]{2,1,0:T(8,128)S(1)}, f32[11,8,128]{2,1,0:T(8,128)S(1)}, u32[]{:S(2)}, u32[]{:S(2)}) collective-permute-start(f32[11,8,128]{2,1,0:T(8,128)S(1)} %get-tuple-element.15.edges), channel_id=1, source_target_pairs={{0,1},{1,0},{2,3},{3,2},{4,5},{5,4},{6,7},{7,6},{8,9},{9,8},{10,11... | collective-permute-start | bytes 135176 | tf_op jit(solution)/shard_map/ppermute | solution.py:407
  12.3 5.8 %collective-permute-start.5 = (f32[22,8,128]{2,1,0:T(8,128)S(1)}, f32[22,8,128]{2,1,0:T(8,128)S(1)}, u32[]{:S(2)}, u32[]{:S(2)}) collective-permute-start(f32[22,8,128]{2,1,0:T(8,128)S(1)} %merge.1.sides), channel_id=1, source_target_pairs={{4,8},{8,4},{12,16},{16,12},{20,24},{24,20},{28,32},{32,28},{36,40... | collective-permute-start | bytes 270344 | tf_op jit(solution)/shard_map/ppermute | solution.py:399
  13.0 6.1 %collective-permute-start.4 = (f32[22,8,128]{2,1,0:T(8,128)S(1)}, f32[22,8,128]{2,1,0:T(8,128)S(1)}, u32[]{:S(2)}, u32[]{:S(2)}) collective-permute-start(f32[22,8,128]{2,1,0:T(8,128)S(1)} %merge.1.sides), channel_id=1, source_target_pairs={{0,4},{4,0},{8,12},{12,8},{16,20},{20,16},{24,28},{28,24},{32,36},... | collective-permute-start | bytes 270344 | tf_op jit(solution)/shard_map/ppermute | solution.py:399
  28.4 2.3 %collective-permute-start.6 = (f32[96,128]{1,0:T(8,128)S(1)}, f32[96,128]{1,0:T(8,128)S(1)}, u32[]{:S(2)}, u32[]{:S(2)}) collective-permute-start(f32[96,128]{1,0:T(8,128)S(1)} %get-tuple-element.18), channel_id=1, source_target_pairs={{0,4},{1,5},{2,6},{3,7},{4,0},{5,1},{6,2},{7,3},{8,12},{9,13},{10,... | collective-permute-start | bytes 147464 | tf_op jit(solution)/shard_map/ppermute | solution.py:412
  30.7 4.1 %collective-permute-start.9 = (f32[96,128]{1,0:T(8,128)S(1)}, f32[96,128]{1,0:T(8,128)S(1)}, u32[]{:S(2)}, u32[]{:S(2)}) collective-permute-start(f32[96,128]{1,0:T(8,128)S(1)} %add.33), channel_id=1, source_target_pairs={{0,3},{1,2},{2,1},{3,0},{4,7},{5,6},{6,5},{7,4},{8,11},{9,10},{10,... | collective-permute-start | bytes 147464 | tf_op jit(solution)/shard_map/ppermute | solution.py:412
  31.3 6.1 %collective-permute-start.8 = (f32[96,128]{1,0:T(8,128)S(1)}, f32[96,128]{1,0:T(8,128)S(1)}, u32[]{:S(2)}, u32[]{:S(2)}) collective-permute-start(f32[96,128]{1,0:T(8,128)S(1)} %add.33), channel_id=1, source_target_pairs={{0,2},{1,3},{2,0},{3,1},{4,6},{5,7},{6,4},{7,5},{8,10},{9,11},{10,... | collective-permute-start | bytes 147464 | tf_op jit(solution)/shard_map/ppermute | solution.py:412
  33.8 4.1 %collective-permute-start.7 = (f32[96,128]{1,0:T(8,128)S(1)}, f32[96,128]{1,0:T(8,128)S(1)}, u32[]{:S(2)}, u32[]{:S(2)}) collective-permute-start(f32[96,128]{1,0:T(8,128)S(1)} %add.33), channel_id=1, source_target_pairs={{0,1},{1,0},{2,3},{3,2},{4,5},{5,4},{6,7},{7,6},{8,9},{9,8},{10,11... | collective-permute-start | bytes 147464 | tf_op jit(solution)/shard_map/ppermute | solution.py:412
  37.9 7.3 %collective-permute-start.12 = (f32[96,128]{1,0:T(8,128)S(1)}, f32[96,128]{1,0:T(8,128)S(1)}, u32[]{:S(2)}, u32[]{:S(2)}) collective-permute-start(f32[96,128]{1,0:T(8,128)S(1)} %add_add_fusion.2), channel_id=1, source_target_pairs={{0,24},{1,25},{2,26},{3,27},{4,28},{5,29},{6,30},{7,31},{8,16},{9,... | collective-permute-start | bytes 147464 | tf_op jit(solution)/shard_map/ppermute | solution.py:412
  43.1 5.6 %collective-permute-start.11 = (f32[96,128]{1,0:T(8,128)S(1)}, f32[96,128]{1,0:T(8,128)S(1)}, u32[]{:S(2)}, u32[]{:S(2)}) collective-permute-start(f32[96,128]{1,0:T(8,128)S(1)} %add_add_fusion.2), channel_id=1, source_target_pairs={{0,16},{1,17},{2,18},{3,19},{4,20},{5,21},{6,22},{7,23},{8,24},{9,... | collective-permute-start | bytes 147464 | tf_op jit(solution)/shard_map/ppermute | solution.py:412
  43.1 5.6 %collective-permute-start.10 = (f32[96,128]{1,0:T(8,128)S(1)}, f32[96,128]{1,0:T(8,128)S(1)}, u32[]{:S(2)}, u32[]{:S(2)}) collective-permute-start(f32[96,128]{1,0:T(8,128)S(1)} %add_add_fusion.2), channel_id=1, source_target_pairs={{0,8},{1,9},{2,10},{3,11},{4,12},{5,13},{6,14},{7,15},{8,0},{9,1},... | collective-permute-start | bytes 147464 | tf_op jit(solution)/shard_map/ppermute | solution.py:412
  48.8 9.3 %collective-permute-start.15 = (f32[96,128]{1,0:T(8,128)S(1)}, f32[96,128]{1,0:T(8,128)S(1)}, u32[]{:S(2)}, u32[]{:S(2)}) collective-permute-start(f32[96,128]{1,0:T(8,128)S(1)} %add_add_fusion.1), channel_id=1, source_target_pairs={{0,96},{1,97},{2,98},{3,99},{4,100},{5,101},{6,102},{7,103},{8,104... | collective-permute-start | bytes 147464 | tf_op jit(solution)/shard_map/ppermute | solution.py:412
  55.9 5.0 %collective-permute-start.14 = (f32[96,128]{1,0:T(8,128)S(1)}, f32[96,128]{1,0:T(8,128)S(1)}, u32[]{:S(2)}, u32[]{:S(2)}) collective-permute-start(f32[96,128]{1,0:T(8,128)S(1)} %add_add_fusion.1), channel_id=1, source_target_pairs={{0,64},{1,65},{2,66},{3,67},{4,68},{5,69},{6,70},{7,71},{8,72},{9,... | collective-permute-start | bytes 147464 | tf_op jit(solution)/shard_map/ppermute | solution.py:412
  55.9 5.0 %collective-permute-start.13 = (f32[96,128]{1,0:T(8,128)S(1)}, f32[96,128]{1,0:T(8,128)S(1)}, u32[]{:S(2)}, u32[]{:S(2)}) collective-permute-start(f32[96,128]{1,0:T(8,128)S(1)} %add_add_fusion.1), channel_id=1, source_target_pairs={{0,32},{1,33},{2,34},{3,35},{4,36},{5,37},{6,38},{7,39},{8,40},{9,... | collective-permute-start | bytes 147464 | tf_op jit(solution)/shard_map/ppermute | solution.py:412
  60.9 5.4 %collective-permute-start.16 = (f32[96,128]{1,0:T(8,128)S(1)}, f32[96,128]{1,0:T(8,128)S(1)}, u32[]{:S(2)}, u32[]{:S(2)}) collective-permute-start(f32[96,128]{1,0:T(8,128)S(1)} %add_add_fusion), channel_id=1, source_target_pairs={{0,224},{1,225},{2,226},{3,227},{4,228},{5,229},{6,230},{7,231},{8... | collective-permute-start | bytes 147464 | tf_op jit(solution)/shard_map/ppermute | solution.py:412

commit v3 on v2

--- a/solution.py
+++ b/solution.py
@@ -102,7 +102,7 @@
                 parts[row, pl.ds(KPREV + at, BLOCK), lanes] = low
         return carry
 
-    lax.fori_loop(0, ROWS, one_row, 0)
+    lax.fori_loop(0, ROWS, one_row, 0, unroll=4)
     token[...] = jnp.zeros_like(token)
 
 

time: 75.4 us -> 75.4 us (level)
  no operation moved by 1% of the time
where the time goes in v3:
time: 75.4 us; the launch traced here: 74.3 us
  starting transfers between devices  31.7 us (42%)
  Pallas kernels  23.2 us (31%)
  waiting for transfers between devices  18.4 us (24%)
  between operations  0.93 us (1%)
    ppermute x11, starting transfers between devices, from_partner(): lax.ppermute(value, ('band', 'col'), [(i, i ^ mask) for i in range(bands...  21.4 us
    ppermute x11, waiting for transfers between devices, from_partner(): lax.ppermute(value, ('band', 'col'), [(i, i ^ mask) for i in range(bands...  16.2 us
    pallas_call x1, Pallas kernels, per_device(): pl.pallas_call(power_kernel, out_shape=(OUT((ROWS, BOTH, COMPS * COLS), b...  9.3 us
    pallas_call x1, Pallas kernels, per_device(): pl.pallas_call(finish_kernel, out_shape=(jax.ShapeDtypeStruct((KPREV, COM...  7.85 us
    ppermute x4, starting transfers between devices, row_exchange(): return lax.ppermute(value, 'band', pairs_in(bands, partner))  6.79 us
    ppermute x2, starting transfers between devices, col_exchange(): return lax.ppermute(value, 'col', pairs_in(cols, partner))  3.49 us
    pallas_call x1, Pallas kernels, per_device(): pl.pallas_call(pack_kernel, out_shape=(OUT((ROWS, SLAB, COLS), f32), OUT(...  3.29 us
    pallas_call x1, Pallas kernels, per_device(): pl.pallas_call(prior_kernel, out_shape=(OUT((ROWS, BOTH, COMPS * COLS), b...  2.71 us
  transfers between devices with their start and end apart: 17, of which 10 were waited for; matrix products, arithmetic and copies ran while one was open for 0% of the time, Pallas kernels for 4%

profile of v3, /device:TPU:2, one launch (start us, length us, event | category | flops | bytes accessed | tf_op | source)
XLA Modules:
  0.0 74.3 jit_solution(8097263172666483797)
XLA Ops:
  0.6 0.0 copy-start
  0.6 3.3 %pack.1 = (f32[8,168,256]{2,1,0:T(8,128)S(1)}, f32[4,168,256]{2,1,0:T(8,128)S(1)}, f32[4,168,256]{2,1,0:T(8,128)S(1)}, f32[11,8,128]{2,1,0:T(8,128)S(1)}) custom-call(f32[8192,128]{1,0:T(8,128)} %bitcast.13, f32[512,128]{1,0:T(8,128)} %bitcast.15, f32[2,8,256]{2,1,0:T(8,128)} %velocity.1), custom_call_target="tpu_custom_call" | custom-call | tf_op jit(solution)/shard_map/pack/pallas_call | solution.py:438
  3.9 0.1 collective-permute-start
  4.0 0.7 collective-permute-start.1
  4.8 3.4 %collective-permute-start.3 = (f32[11,8,128]{2,1,0:T(8,128)S(1)}, f32[11,8,128]{2,1,0:T(8,128)S(1)}, u32[]{:S(2)}, u32[]{:S(2)}) collective-permute-start(f32[11,8,128]{2,1,0:T(8,128)S(1)} %get-tuple-element.15.edges), channel_id=1, source_target_pairs={{1,2},{2,1},{5,6},{6,5},{9,10},{10,9},{13,14},{14,13},{17,18},{18,... | collective-permute-start | bytes 135176 | tf_op jit(solution)/shard_map/ppermute | solution.py:407
  8.2 0.1 collective-permute-start.2
  8.3 0.0 copy-done
  8.3 2.7 %prior.1 = (bf16[8,128,2048]{2,1,0:T(8,128)(2,1)S(1)}, f32[8,128]{1,0:T(8,128)S(1)}) custom-call(f32[8192,128]{1,0:T(8,128)S(1)} %bitcast.14), custom_call_target="tpu_custom_call" | custom-call | flops 4000000000 | bytes 8000000 | tf_op jit(solution)/shard_map/prior/pallas_call | solution.py:464
  11.0 0.0 collective-permute-done.3.side_odd
  11.0 1.3 %collective-permute-done.2.side_even = f32[11,8,128]{2,1,0:T(8,128)S(1)} collective-permute-done((f32[11,8,128]{2,1,0:T(8,128)S(1)}, f32[11,8,128]{2,1,0:T(8,128)S(1)}, u32[]{:S(2)}, u32[]{:S(2)}) %collective-permute-start.2) | collective-permute-done | bytes 45088 | tf_op jit(solution)/shard_map/ppermute | solution.py:407
  12.3 0.7 collective-permute-start.5
  13.0 5.3 %collective-permute-start.4 = (f32[22,8,128]{2,1,0:T(8,128)S(1)}, f32[22,8,128]{2,1,0:T(8,128)S(1)}, u32[]{:S(2)}, u32[]{:S(2)}) collective-permute-start(f32[22,8,128]{2,1,0:T(8,128)S(1)} %merge.1.sides), channel_id=1, source_target_pairs={{0,4},{4,0},{8,12},{12,8},{16,20},{20,16},{24,28},{28,24},{32,36},... | collective-permute-start | bytes 270344 | tf_op jit(solution)/shard_map/ppermute | solution.py:399
  18.3 0.0 collective-permute-done.5.chip_sides
  18.3 0.9 %collective-permute-done.4.core_sides = f32[22,8,128]{2,1,0:T(8,128)S(1)} collective-permute-done((f32[22,8,128]{2,1,0:T(8,128)S(1)}, f32[22,8,128]{2,1,0:T(8,128)S(1)}, u32[]{:S(2)}, u32[]{:S(2)}) %collective-permute-start.4) | collective-permute-done | bytes 90144 | tf_op jit(solution)/shard_map/ppermute | solution.py:399
  19.3 0.0 collective-permute-done.from_core
  19.3 0.0 collective-permute-done.1.from_chip
  19.3 9.3 %powers.1 = (bf16[8,128,2048]{2,1,0:T(8,128)(2,1)S(1)}, f32[96,128]{1,0:T(8,128)S(1)}) custom-call(f32[8,168,256]{2,1,0:T(8,128)S(1)} %get-tuple-element.12.slab, f32[4,168,256]{2,1,0:T(8,128)S(1)} %collective-permute-done.from_core, f32[4,168,256]{2,1,0:T(8,128)S(1)} %collective-permute-done.1.from_chip, f32[22,8,128]{2,1,0:T(8,128)S(1)} %merge.1.sides, ...), custom_call_target="tpu_custom_call" | custom-call | tf_op jit(solution)/shard_map/powers/pallas_call | solution.py:486
  28.6 1.1 %collective-permute-start.6 = (f32[96,128]{1,0:T(8,128)S(1)}, f32[96,128]{1,0:T(8,128)S(1)}, u32[]{:S(2)}, u32[]{:S(2)}) collective-permute-start(f32[96,128]{1,0:T(8,128)S(1)} %get-tuple-element.18), channel_id=1, source_target_pairs={{0,4},{1,5},{2,6},{3,7},{4,0},{5,1},{6,2},{7,3},{8,12},{9,13},{10,... | collective-permute-start | bytes 147464 | tf_op jit(solution)/shard_map/ppermute | solution.py:412
  29.7 0.9 %collective-permute-done.6 = f32[96,128]{1,0:T(8,128)S(1)} collective-permute-done((f32[96,128]{1,0:T(8,128)S(1)}, f32[96,128]{1,0:T(8,128)S(1)}, u32[]{:S(2)}, u32[]{:S(2)}) %collective-permute-start.6) | collective-permute-done | bytes 49184 | tf_op jit(solution)/shard_map/ppermute | solution.py:412
  30.6 0.5 collective-permute-start.9
  31.1 2.5 %collective-permute-start.8 = (f32[96,128]{1,0:T(8,128)S(1)}, f32[96,128]{1,0:T(8,128)S(1)}, u32[]{:S(2)}, u32[]{:S(2)}) collective-permute-start(f32[96,128]{1,0:T(8,128)S(1)} %add.33), channel_id=1, source_target_pairs={{0,2},{1,3},{2,0},{3,1},{4,6},{5,7},{6,4},{7,5},{8,10},{9,11},{10,... | collective-permute-start | bytes 147464 | tf_op jit(solution)/shard_map/ppermute | solution.py:412
  33.6 1.1 %collective-permute-start.7 = (f32[96,128]{1,0:T(8,128)S(1)}, f32[96,128]{1,0:T(8,128)S(1)}, u32[]{:S(2)}, u32[]{:S(2)}) collective-permute-start(f32[96,128]{1,0:T(8,128)S(1)} %add.33), channel_id=1, source_target_pairs={{0,1},{1,0},{2,3},{3,2},{4,5},{5,4},{6,7},{7,6},{8,9},{9,8},{10,11... | collective-permute-start | bytes 147464 | tf_op jit(solution)/shard_map/ppermute | solution.py:412
  34.7 0.0 collective-permute-done.9
  34.7 2.4 %collective-permute-done.8 = f32[96,128]{1,0:T(8,128)S(1)} collective-permute-done((f32[96,128]{1,0:T(8,128)S(1)}, f32[96,128]{1,0:T(8,128)S(1)}, u32[]{:S(2)}, u32[]{:S(2)}) %collective-permute-start.8) | collective-permute-done | bytes 49184 | tf_op jit(solution)/shard_map/ppermute | solution.py:412
  37.1 0.6 collective-permute-done.7
  37.7 5.2 %collective-permute-start.12 = (f32[96,128]{1,0:T(8,128)S(1)}, f32[96,128]{1,0:T(8,128)S(1)}, u32[]{:S(2)}, u32[]{:S(2)}) collective-permute-start(f32[96,128]{1,0:T(8,128)S(1)} %add_add_fusion.2), channel_id=1, source_target_pairs={{0,24},{1,25},{2,26},{3,27},{4,28},{5,29},{6,30},{7,31},{8,16},{9,... | collective-permute-start | bytes 147464 | tf_op jit(solution)/shard_map/ppermute | solution.py:412
  42.9 0.0 collective-permute-start.11
  42.9 1.0 %collective-permute-start.10 = (f32[96,128]{1,0:T(8,128)S(1)}, f32[96,128]{1,0:T(8,128)S(1)}, u32[]{:S(2)}, u32[]{:S(2)}) collective-permute-start(f32[96,128]{1,0:T(8,128)S(1)} %add_add_fusion.2), channel_id=1, source_target_pairs={{0,8},{1,9},{2,10},{3,11},{4,12},{5,13},{6,14},{7,15},{8,0},{9,1},... | collective-permute-start | bytes 147464 | tf_op jit(solution)/shard_map/ppermute | solution.py:412
  43.9 1.1 %collective-permute-done.12 = f32[96,128]{1,0:T(8,128)S(1)} collective-permute-done((f32[96,128]{1,0:T(8,128)S(1)}, f32[96,128]{1,0:T(8,128)S(1)}, u32[]{:S(2)}, u32[]{:S(2)}) %collective-permute-start.12) | collective-permute-done | bytes 49184 | tf_op jit(solution)/shard_map/ppermute | solution.py:412
  45.0 3.5 %collective-permute-done.11 = f32[96,128]{1,0:T(8,128)S(1)} collective-permute-done((f32[96,128]{1,0:T(8,128)S(1)}, f32[96,128]{1,0:T(8,128)S(1)}, u32[]{:S(2)}, u32[]{:S(2)}) %collective-permute-start.11) | collective-permute-done | bytes 49184 | tf_op jit(solution)/shard_map/ppermute | solution.py:412
  48.5 0.0 collective-permute-done.10
  48.5 7.4 %collective-permute-start.15 = (f32[96,128]{1,0:T(8,128)S(1)}, f32[96,128]{1,0:T(8,128)S(1)}, u32[]{:S(2)}, u32[]{:S(2)}) collective-permute-start(f32[96,128]{1,0:T(8,128)S(1)} %add_add_fusion.1), channel_id=1, source_target_pairs={{0,96},{1,97},{2,98},{3,99},{4,100},{5,101},{6,102},{7,103},{8,104... | collective-permute-start | bytes 147464 | tf_op jit(solution)/shard_map/ppermute | solution.py:412
  55.9 0.0 collective-permute-start.14
  55.9 0.7 collective-permute-start.13
  56.6 1.4 %collective-permute-done.15 = f32[96,128]{1,0:T(8,128)S(1)} collective-permute-done((f32[96,128]{1,0:T(8,128)S(1)}, f32[96,128]{1,0:T(8,128)S(1)}, u32[]{:S(2)}, u32[]{:S(2)}) %collective-permute-start.15) | collective-permute-done | bytes 49184 | tf_op jit(solution)/shard_map/ppermute | solution.py:412
  58.0 2.9 %collective-permute-done.14 = f32[96,128]{1,0:T(8,128)S(1)} collective-permute-done((f32[96,128]{1,0:T(8,128)S(1)}, f32[96,128]{1,0:T(8,128)S(1)}, u32[]{:S(2)}, u32[]{:S(2)}) %collective-permute-start.14) | collective-permute-done | bytes 49184 | tf_op jit(solution)/shard_map/ppermute | solution.py:412
  60.9 0.0 collective-permute-done.13
  60.9 2.1 %collective-permute-start.16 = (f32[96,128]{1,0:T(8,128)S(1)}, f32[96,128]{1,0:T(8,128)S(1)}, u32[]{:S(2)}, u32[]{:S(2)}) collective-permute-start(f32[96,128]{1,0:T(8,128)S(1)} %add_add_fusion), channel_id=1, source_target_pairs={{0,224},{1,225},{2,226},{3,227},{4,228},{5,229},{6,230},{7,231},{8... | collective-permute-start | bytes 147464 | tf_op jit(solution)/shard_map/ppermute | solution.py:412
  63.0 3.3 %collective-permute-done.16 = f32[96,128]{1,0:T(8,128)S(1)} collective-permute-done((f32[96,128]{1,0:T(8,128)S(1)}, f32[96,128]{1,0:T(8,128)S(1)}, u32[]{:S(2)}, u32[]{:S(2)}) %collective-permute-start.16) | collective-permute-done | bytes 49184 | tf_op jit(solution)/shard_map/ppermute | solution.py:412
  66.3 7.9 %finish.1 = (f32[64,8,2,8,128]{4,3,2,1,0:T(8,128)}, f32[64,64]{1,0:T(8,128)}) custom-call(f32[96,128]{1,0:T(8,128)S(1)} %add.43.inner, bf16[8,128,2048]{2,1,0:T(8,128)(2,1)S(1)} %get-tuple-element.17.prior_parts, bf16[8,128,2048]{2,1,0:T(8,128)(2,1)S(1)} %get-tuple-element.19.new_parts), custom_call_target="tpu_custom_call" | custom-call | tf_op jit(solution)/shard_map/finish/pallas_call | solution.py:509
  (6 shorter events, 0.1 us)
Async XLA Ops:
  0.6 7.6 %copy-start = (f32[64,2,4,8,256]{4,3,2,1,0:T(8,128)S(1)}, f32[64,2,4,8,256]{4,3,2,1,0:T(8,128)}, u32[]{:S(2)}) copy-start(f32[64,2,4,8,256]{4,3,2,1,0:T(8,128)} %param.3) | copy-start | bytes 12582916
  3.9 15.3 %collective-permute-start = (f32[4,168,256]{2,1,0:T(8,128)S(1)}, f32[4,168,256]{2,1,0:T(8,128)S(1)}, u32[]{:S(2)}, u32[]{:S(2)}) collective-permute-start(f32[4,168,256]{2,1,0:T(8,128)S(1)} %get-tuple-element.13), channel_id=1, source_target_pairs={{0,4},{4,0},{8,12},{12,8},{16,20},{20,16},{24,28},{28,24},{32,36},... | collective-permute-start | bytes 2064392 | tf_op jit(solution)/shard_map/ppermute | solution.py:399
  4.0 15.2 %collective-permute-start.1 = (f32[4,168,256]{2,1,0:T(8,128)S(1)}, f32[4,168,256]{2,1,0:T(8,128)S(1)}, u32[]{:S(2)}, u32[]{:S(2)}) collective-permute-start(f32[4,168,256]{2,1,0:T(8,128)S(1)} %get-tuple-element.14), channel_id=1, source_target_pairs={{4,8},{8,4},{12,16},{16,12},{20,24},{24,20},{28,32},{32,28},{36,40... | collective-permute-start | bytes 2064392 | tf_op jit(solution)/shard_map/ppermute | solution.py:399
  4.8 6.2 %collective-permute-start.3 = (f32[11,8,128]{2,1,0:T(8,128)S(1)}, f32[11,8,128]{2,1,0:T(8,128)S(1)}, u32[]{:S(2)}, u32[]{:S(2)}) collective-permute-start(f32[11,8,128]{2,1,0:T(8,128)S(1)} %get-tuple-element.15.edges), channel_id=1, source_target_pairs={{1,2},{2,1},{5,6},{6,5},{9,10},{10,9},{13,14},{14,13},{17,18},{18,... | collective-permute-start | bytes 135176 | tf_op jit(solution)/shard_map/ppermute | solution.py:407
  8.2 4.1 %collective-permute-start.2 = (f32[11,8,128]{2,1,0:T(8,128)S(1)}, f32[11,8,128]{2,1,0:T(8,128)S(1)}, u32[]{:S(2)}, u32[]{:S(2)}) collective-permute-start(f32[11,8,128]{2,1,0:T(8,128)S(1)} %get-tuple-element.15.edges), channel_id=1, source_target_pairs={{0,1},{1,0},{2,3},{3,2},{4,5},{5,4},{6,7},{7,6},{8,9},{9,8},{10,11... | collective-permute-start | bytes 135176 | tf_op jit(solution)/shard_map/ppermute | solution.py:407
  12.3 6.0 %collective-permute-start.5 = (f32[22,8,128]{2,1,0:T(8,128)S(1)}, f32[22,8,128]{2,1,0:T(8,128)S(1)}, u32[]{:S(2)}, u32[]{:S(2)}) collective-permute-start(f32[22,8,128]{2,1,0:T(8,128)S(1)} %merge.1.sides), channel_id=1, source_target_pairs={{4,8},{8,4},{12,16},{16,12},{20,24},{24,20},{28,32},{32,28},{36,40... | collective-permute-start | bytes 270344 | tf_op jit(solution)/shard_map/ppermute | solution.py:399
  13.0 6.3 %collective-permute-start.4 = (f32[22,8,128]{2,1,0:T(8,128)S(1)}, f32[22,8,128]{2,1,0:T(8,128)S(1)}, u32[]{:S(2)}, u32[]{:S(2)}) collective-permute-start(f32[22,8,128]{2,1,0:T(8,128)S(1)} %merge.1.sides), channel_id=1, source_target_pairs={{0,4},{4,0},{8,12},{12,8},{16,20},{20,16},{24,28},{28,24},{32,36},... | collective-permute-start | bytes 270344 | tf_op jit(solution)/shard_map/ppermute | solution.py:399
  28.6 2.0 %collective-permute-start.6 = (f32[96,128]{1,0:T(8,128)S(1)}, f32[96,128]{1,0:T(8,128)S(1)}, u32[]{:S(2)}, u32[]{:S(2)}) collective-permute-start(f32[96,128]{1,0:T(8,128)S(1)} %get-tuple-element.18), channel_id=1, source_target_pairs={{0,4},{1,5},{2,6},{3,7},{4,0},{5,1},{6,2},{7,3},{8,12},{9,13},{10,... | collective-permute-start | bytes 147464 | tf_op jit(solution)/shard_map/ppermute | solution.py:412
  30.6 4.1 %collective-permute-start.9 = (f32[96,128]{1,0:T(8,128)S(1)}, f32[96,128]{1,0:T(8,128)S(1)}, u32[]{:S(2)}, u32[]{:S(2)}) collective-permute-start(f32[96,128]{1,0:T(8,128)S(1)} %add.33), channel_id=1, source_target_pairs={{0,3},{1,2},{2,1},{3,0},{4,7},{5,6},{6,5},{7,4},{8,11},{9,10},{10,... | collective-permute-start | bytes 147464 | tf_op jit(solution)/shard_map/ppermute | solution.py:412
  31.1 6.0 %collective-permute-start.8 = (f32[96,128]{1,0:T(8,128)S(1)}, f32[96,128]{1,0:T(8,128)S(1)}, u32[]{:S(2)}, u32[]{:S(2)}) collective-permute-start(f32[96,128]{1,0:T(8,128)S(1)} %add.33), channel_id=1, source_target_pairs={{0,2},{1,3},{2,0},{3,1},{4,6},{5,7},{6,4},{7,5},{8,10},{9,11},{10,... | collective-permute-start | bytes 147464 | tf_op jit(solution)/shard_map/ppermute | solution.py:412
  33.6 4.1 %collective-permute-start.7 = (f32[96,128]{1,0:T(8,128)S(1)}, f32[96,128]{1,0:T(8,128)S(1)}, u32[]{:S(2)}, u32[]{:S(2)}) collective-permute-start(f32[96,128]{1,0:T(8,128)S(1)} %add.33), channel_id=1, source_target_pairs={{0,1},{1,0},{2,3},{3,2},{4,5},{5,4},{6,7},{7,6},{8,9},{9,8},{10,11... | collective-permute-start | bytes 147464 | tf_op jit(solution)/shard_map/ppermute | solution.py:412
  37.7 7.3 %collective-permute-start.12 = (f32[96,128]{1,0:T(8,128)S(1)}, f32[96,128]{1,0:T(8,128)S(1)}, u32[]{:S(2)}, u32[]{:S(2)}) collective-permute-start(f32[96,128]{1,0:T(8,128)S(1)} %add_add_fusion.2), channel_id=1, source_target_pairs={{0,24},{1,25},{2,26},{3,27},{4,28},{5,29},{6,30},{7,31},{8,16},{9,... | collective-permute-start | bytes 147464 | tf_op jit(solution)/shard_map/ppermute | solution.py:412
  42.9 5.6 %collective-permute-start.11 = (f32[96,128]{1,0:T(8,128)S(1)}, f32[96,128]{1,0:T(8,128)S(1)}, u32[]{:S(2)}, u32[]{:S(2)}) collective-permute-start(f32[96,128]{1,0:T(8,128)S(1)} %add_add_fusion.2), channel_id=1, source_target_pairs={{0,16},{1,17},{2,18},{3,19},{4,20},{5,21},{6,22},{7,23},{8,24},{9,... | collective-permute-start | bytes 147464 | tf_op jit(solution)/shard_map/ppermute | solution.py:412
  42.9 5.6 %collective-permute-start.10 = (f32[96,128]{1,0:T(8,128)S(1)}, f32[96,128]{1,0:T(8,128)S(1)}, u32[]{:S(2)}, u32[]{:S(2)}) collective-permute-start(f32[96,128]{1,0:T(8,128)S(1)} %add_add_fusion.2), channel_id=1, source_target_pairs={{0,8},{1,9},{2,10},{3,11},{4,12},{5,13},{6,14},{7,15},{8,0},{9,1},... | collective-permute-start | bytes 147464 | tf_op jit(solution)/shard_map/ppermute | solution.py:412
  48.5 9.4 %collective-permute-start.15 = (f32[96,128]{1,0:T(8,128)S(1)}, f32[96,128]{1,0:T(8,128)S(1)}, u32[]{:S(2)}, u32[]{:S(2)}) collective-permute-start(f32[96,128]{1,0:T(8,128)S(1)} %add_add_fusion.1), channel_id=1, source_target_pairs={{0,96},{1,97},{2,98},{3,99},{4,100},{5,101},{6,102},{7,103},{8,104... | collective-permute-start | bytes 147464 | tf_op jit(solution)/shard_map/ppermute | solution.py:412
  55.9 5.0 %collective-permute-start.14 = (f32[96,128]{1,0:T(8,128)S(1)}, f32[96,128]{1,0:T(8,128)S(1)}, u32[]{:S(2)}, u32[]{:S(2)}) collective-permute-start(f32[96,128]{1,0:T(8,128)S(1)} %add_add_fusion.1), channel_id=1, source_target_pairs={{0,64},{1,65},{2,66},{3,67},{4,68},{5,69},{6,70},{7,71},{8,72},{9,... | collective-permute-start | bytes 147464 | tf_op jit(solution)/shard_map/ppermute | solution.py:412
  55.9 5.0 %collective-permute-start.13 = (f32[96,128]{1,0:T(8,128)S(1)}, f32[96,128]{1,0:T(8,128)S(1)}, u32[]{:S(2)}, u32[]{:S(2)}) collective-permute-start(f32[96,128]{1,0:T(8,128)S(1)} %add_add_fusion.1), channel_id=1, source_target_pairs={{0,32},{1,33},{2,34},{3,35},{4,36},{5,37},{6,38},{7,39},{8,40},{9,... | collective-permute-start | bytes 147464 | tf_op jit(solution)/shard_map/ppermute | solution.py:412
  60.9 5.4 %collective-permute-start.16 = (f32[96,128]{1,0:T(8,128)S(1)}, f32[96,128]{1,0:T(8,128)S(1)}, u32[]{:S(2)}, u32[]{:S(2)}) collective-permute-start(f32[96,128]{1,0:T(8,128)S(1)} %add_add_fusion), channel_id=1, source_target_pairs={{0,224},{1,225},{2,226},{3,227},{4,228},{5,229},{6,230},{7,231},{8... | collective-permute-start | bytes 147464 | tf_op jit(solution)/shard_map/ppermute | solution.py:412
